TPU v7x, 512 devices: a whole 4x8x8 slice. The times are simulated.
512 devices in a mesh: gx: 16 (over y, core), gy: 32 (over x, z).
Axes of the slice: x: 4, y: 8, z: 8, core: 2. Of those that a mesh axis runs over, the one named last changes fastest.
Arguments:
- head_before: float32 [8, 256, 32768], P(None, 'gx', 'gy'), may hold values from -6 to 6
- log_conductivity: float32 [256, 32768], P('gx', 'gy'), may hold values from -2.5 to 2.5
- fixed_mask: int32 [256, 32768], P('gx', 'gy'), may hold values 0 or 1
- well_cells: int32 [8], replicated, may hold values from 0 to 8388607
- pump_rates: float32 [8], replicated, may hold values from 50 to 500
- adjoint_seed: float32 [8, 256, 32768], P(None, 'gx', 'gy'), may hold values from -6 to 6
Outputs:
- heads: float32 [8, 256, 32768], P(None, 'gx', 'gy')
- conductivity_sensitivity: float32 [256, 32768], P('gx', 'gy')
All inputs are finite; a program needn't handle non-finite values. No bound on the sum of `fixed_mask` on one device may be relied on, other than what follows from the above.
Results may differ from a plain program's by a relative error of at most 0.00045.
Values sent between devices are 32-bit elements; how exact they have to be, the bound alone decides.
No kernel may reach another device: no remote copies, remote signals or barrier semaphores. Data moves between devices by JAX's collectives and lax.ppermute only.
A program may use at most 64 MiB of HBM per device.

v0:
```python
import jax
import jax.numpy as jnp
from jax import lax
from jax.sharding import PartitionSpec as P

implicit_ratio = 4000.0
explicit_ratio = 0.1


def shifted(x, axis, by):
    peers = lax.axis_size(axis)
    pairs = [(i, i + by) for i in range(peers) if 0 <= i + by < peers]
    return lax.ppermute(x, axis, pairs)


def padded(cells, sides, width):
    for axis, dim in sides:
        count = lax.axis_size(axis)
        ends = count - 1
        head = lax.slice_in_dim(cells, 0, width, axis=dim)
        tail = lax.slice_in_dim(cells, cells.shape[dim] - width, cells.shape[dim], axis=dim)
        cells = jnp.concatenate(
            [
                lax.ppermute(tail, axis, [(i, (i + 1) % count) for i in range(ends)]),
                cells,
                lax.ppermute(head, axis, [((i + 1) % count, i) for i in range(ends)]),
            ],
            axis=dim,
        )
    return cells


def harmonic(own_value, other_value):
    return 2.0 * own_value * other_value / (own_value + other_value)


def face_slope(own_value, other_value):
    summed = own_value + other_value
    return 2.0 * own_value * other_value * other_value / (summed * summed)


def blank_rows(template):
    nothing = jnp.zeros_like(template)
    return jnp.concatenate(
        [nothing[:, 0:1], jnp.ones_like(nothing[:, 1:2]), nothing[:, 2:]], axis=1
    )


def reduce_level(current, lower_rows, upper_rows):
    left_factor = current[:, 0:1] / lower_rows[:, 1:2]
    right_factor = current[:, 2:3] / upper_rows[:, 1:2]
    new_lower = -left_factor * lower_rows[:, 0:1]
    new_upper = -right_factor * upper_rows[:, 2:3]
    new_middle = (
        current[:, 1:2] - left_factor * lower_rows[:, 2:3] - right_factor * upper_rows[:, 0:1]
    )
    new_rhs = current[:, 3:] - left_factor * lower_rows[:, 3:] - right_factor * upper_rows[:, 3:]
    return jnp.concatenate([new_lower, new_middle, new_upper, new_rhs], axis=1)


def local_sweep(packed):
    length = packed.shape[2]
    stride = 1
    while stride < length:
        filler = blank_rows(packed[:, :, :stride])
        lower_rows = jnp.concatenate([filler, packed[:, :, : length - stride]], axis=2)
        upper_rows = jnp.concatenate([packed[:, :, stride:], filler], axis=2)
        packed = reduce_level(packed, lower_rows, upper_rows)
        stride = stride * 2
    return packed[:, 3:] / packed[:, 1:2]


def line_solve(coefficients, right_side):
    test_count = right_side.shape[1]
    row_count = coefficients.shape[2]
    last_row = row_count - 1
    row_ids = lax.broadcasted_iota(jnp.int32, (1, 1, row_count, 1), 2)
    inside = row_ids < last_row
    inner_lower = jnp.where((row_ids > 0) & inside, coefficients[:, 0:1], 0.0)
    inner_upper = jnp.where(row_ids < last_row - 1, coefficients[:, 2:3], 0.0)
    inner_middle = jnp.where(inside, coefficients[:, 1:2], 1.0)
    inner_rhs = jnp.where(inside, right_side, 0.0)
    left_source = jnp.where(row_ids == 0, -coefficients[:, 0:1], 0.0)
    right_source = jnp.where(row_ids == last_row - 1, -coefficients[:, 2:3], 0.0)
    packed = jnp.concatenate(
        [inner_lower, inner_middle, inner_upper, inner_rhs, left_source, right_source], axis=1
    )
    solved = local_sweep(packed)
    first_rows = solved[:, :, 0]
    next_first = shifted(first_rows, "gx", -1)
    last_lower = coefficients[:, 0:1, last_row]
    last_middle = coefficients[:, 1:2, last_row]
    last_upper = coefficients[:, 2:3, last_row]
    last_rhs = right_side[:, :, last_row]
    prev_base = solved[:, :test_count, last_row - 1]
    prev_left = solved[:, test_count : test_count + 1, last_row - 1]
    prev_right = solved[:, test_count + 1 :, last_row - 1]
    next_base = next_first[:, :test_count]
    next_left = next_first[:, test_count : test_count + 1]
    next_right = next_first[:, test_count + 1 :]
    reduced = jnp.concatenate(
        [
            last_lower * prev_left,
            last_middle + last_lower * prev_right + last_upper * next_left,
            last_upper * next_right,
            last_rhs - last_lower * prev_base - last_upper * next_base,
        ],
        axis=1,
    )
    position = lax.axis_index("gx")
    line_devices = lax.axis_size("gx")
    identity_rows = blank_rows(reduced)
    stride = 1
    while stride < line_devices:
        below_rows = shifted(reduced, "gx", stride)
        above_rows = shifted(reduced, "gx", -stride)
        below_rows = below_rows + identity_rows * (position < stride).astype(jnp.float32)
        above_rows = above_rows + identity_rows * (position >= line_devices - stride).astype(
            jnp.float32
        )
        reduced = reduce_level(reduced, below_rows, above_rows)
        stride = stride * 2
    separator = reduced[:, 3:] / reduced[:, 1:2]
    prior_separator = shifted(separator, "gx", 1)
    solution = (
        solved[:, :test_count]
        + solved[:, test_count : test_count + 1] * prior_separator[:, :, None]
        + solved[:, test_count + 1 :] * separator[:, :, None]
    )
    return jnp.concatenate([solution[:, :, :last_row], separator[:, :, None]], axis=2)


def per_device(head_before, log_conductivity, fixed_mask, well_cells, pump_rates, adjoint_seed):
    test_count, row_count, column_count = head_before.shape
    active = (1 - fixed_mask).astype(jnp.float32)
    conduct = jnp.exp(log_conductivity)
    bordered = padded(jnp.stack([conduct, active]), (("gx", 1), ("gy", 2)), 1)
    cond_pad = bordered[0]
    act_pad = bordered[1]
    west_cond = cond_pad[:-2, 1:-1]
    east_cond = cond_pad[2:, 1:-1]
    south_cond = cond_pad[1:-1, :-2]
    north_cond = cond_pad[1:-1, 2:]
    west_act = act_pad[:-2, 1:-1]
    east_act = act_pad[2:, 1:-1]
    south_act = act_pad[1:-1, :-2]
    north_act = act_pad[1:-1, 2:]
    west_face = harmonic(conduct, west_cond)
    east_face = harmonic(conduct, east_cond)
    south_face = harmonic(conduct, south_cond)
    north_face = harmonic(conduct, north_cond)
    head_pad = padded(head_before, (("gy", 2),), 1)
    spread = north_face * (head_pad[:, :, 2:] - head_before) + south_face * (
        head_pad[:, :, :-2] - head_before
    )
    total_columns = column_count * lax.axis_size("gy")
    row_start = lax.axis_index("gx") * row_count
    column_start = lax.axis_index("gy") * column_count
    global_rows = row_start + lax.broadcasted_iota(jnp.int32, (1, row_count, 1), 1)
    global_columns = column_start + lax.broadcasted_iota(jnp.int32, (1, 1, column_count), 2)
    well_row = (well_cells // total_columns)[:, None, None]
    well_column = (well_cells % total_columns)[:, None, None]
    well_here = (well_row == global_rows) & (well_column == global_columns)
    source = jnp.where(well_here, pump_rates[:, None, None], 0.0)
    right_side = head_before + active * (explicit_ratio * spread + source)
    middle = 1.0 + implicit_ratio * (west_face + east_face) * active
    forward_coefficients = jnp.stack(
        [-implicit_ratio * west_face * active, middle, -implicit_ratio * east_face * active]
    )[None]
    adjoint_coefficients = jnp.stack(
        [-implicit_ratio * west_face * west_act, middle, -implicit_ratio * east_face * east_act]
    )[None]
    heads = line_solve(forward_coefficients, right_side[None])[0]
    adjoint_field = line_solve(adjoint_coefficients, adjoint_seed[None])[0]
    row_pad = padded(jnp.stack([heads, adjoint_field]), (("gx", 2),), 1)
    heads_pad = row_pad[0]
    adj_rows = row_pad[1]
    adj_cols = padded(adjoint_field, (("gy", 2),), 1)
    own_weight = adjoint_field * active
    west_term = jnp.sum(
        (heads_pad[:, :-2] - heads) * (own_weight - adj_rows[:, :-2] * west_act), axis=0
    )
    east_term = jnp.sum(
        (heads_pad[:, 2:] - heads) * (own_weight - adj_rows[:, 2:] * east_act), axis=0
    )
    south_term = jnp.sum(
        (head_pad[:, :, :-2] - head_before) * (own_weight - adj_cols[:, :, :-2] * south_act), axis=0
    )
    north_term = jnp.sum(
        (head_pad[:, :, 2:] - head_before) * (own_weight - adj_cols[:, :, 2:] * north_act), axis=0
    )
    sensitivity = implicit_ratio * (
        west_term * face_slope(conduct, west_cond) + east_term * face_slope(conduct, east_cond)
    )
    sensitivity = sensitivity + explicit_ratio * (
        south_term * face_slope(conduct, south_cond) + north_term * face_slope(conduct, north_cond)
    )
    return (heads, sensitivity)


def solution(mesh):
    return jax.shard_map(
        per_device,
        mesh=mesh,
        in_specs=(P(None, "gx", "gy"), P("gx", "gy"), P("gx", "gy"), P(), P(), P(None, "gx", "gy")),
        out_specs=(P(None, "gx", "gy"), P("gx", "gy")),
        check_vma=False,
    )
```

profile of v0, /device:TPU:7, one launch (start us, length us, event | category | flops | bytes accessed | tf_op | source)
XLA Modules:
  0.0 186.0 jit_solution(1346518093609499870)
XLA Ops:
  2.4 3.8 %collective-permute-start = (f32[2,1,1024]{2,1,0:T(1,128)S(1)}, f32[2,1,1024]{2,1,0:T(1,128)S(1)}, u32[]{:S(2)}, u32[]{:S(2)}) collective-permute-start(f32[2,1,1024]{2,1,0:T(1,128)S(1)} %get-tuple-element.153), channel_id=1, source_target_pairs={{0,32},{32,64},{64,96},{96,128},{128,160},{160,192},{192,224},{224... | collective-permute-start | bytes 24584 | tf_op jit(solution)/shard_map/ppermute | solution.py:24
  9.1 10.9 %collective-permute-start.4 = (f32[8,16,1]{2,1,0:T(8,128)S(1)}, f32[8,16,1]{2,1,0:T(8,128)S(1)}, u32[]{:S(2)}, u32[]{:S(2)}) collective-permute-start(f32[8,16,1]{2,1,0:T(8,128)S(1)} %get-tuple-element.113), channel_id=1, source_target_pairs={{1,0},{2,1},{3,2},{4,3},{5,4},{6,5},{7,6},{8,7},{9,8},{10,9},{11,1... | collective-permute-start | bytes 1544 | tf_op jit(solution)/shard_map/ppermute | solution.py:26
  26.4 5.5 %collective-permute-start.3 = (f32[2,18,1]{2,1,0:T(8,128)S(1)}, f32[2,18,1]{2,1,0:T(8,128)S(1)}, u32[]{:S(2)}, u32[]{:S(2)}) collective-permute-start(f32[2,18,1]{2,1,0:T(8,128)S(1)} %get-tuple-element.145), channel_id=1, source_target_pairs={{1,0},{2,1},{3,2},{4,3},{5,4},{6,5},{7,6},{8,7},{9,8},{10,9},{11,1... | collective-permute-start | bytes 440 | tf_op jit(solution)/shard_map/ppermute | solution.py:26
  40.6 3.2 %fusion.14 = (f32[1,10,16,1024]{3,0,2,1:T(1,128)S(1)}, f32[1,10,16,1024]{3,0,2,1:T(1,128)S(1)}) fusion(f32[1,1,16,1024]{3,0,2,1:T(1,128)S(1)} %get-tuple-element.82, f32[1,1,16,1024]{3,0,2,1:T(1,128)S(1)} %get-tuple-element.84, f32[1,8,16,1024]{3,0,2,1:T(1,128)S(1)} %select_n.64, f32[16,1024]{1,0:T(8,128)S(1)} %bitcast.192, f32[16,1024]{1,0:T(8,128)S(1)} %bitcast.194, ...), kind=kLoop, calls=%fused_computation.62 | loop fusion | flops 2621440 | bytes 6131712 | tf_op jit(solution)/shard_map/sub | solution.py:57
  48.8 2.5 %fusion.12 = (f32[1,10,16,1024]{3,0,2,1:T(1,128)S(1)}, f32[1,10,16,1024]{3,0,2,1:T(1,128)S(1)}) fusion(f32[1,10,16,1024]{3,0,2,1:T(1,128)S(1)} %get-tuple-element.169, f32[16,1024]{1,0:T(8,128)S(1)} %bitcast.196, f32[16,1024]{1,0:T(8,128)S(1)} %bitcast.200, f32[1,13,2,1024]{3,0,2,1:T(1,128)S(1)} %copy-done.2, f32[1,13,14,1024]{3,0,2,1:T(1,128)S(1)} %get-tuple-element.95, ...), kind=kLoop, calls=%fused_computation.58 | loop fusion | flops 1966080 | bytes 5971968 | tf_op jit(solution)/shard_map/sub | solution.py:57
  56.8 2.9 %fusion.10 = (f32[1,10,16,1024]{3,0,2,1:T(1,128)S(1)}, f32[1,10,16,1024]{3,0,2,1:T(1,128)S(1)}) fusion(f32[1,10,16,1024]{3,0,2,1:T(1,128)S(1)} %get-tuple-element.161, f32[16,1024]{1,0:T(8,128)S(1)} %bitcast.197, f32[16,1024]{1,0:T(8,128)S(1)} %bitcast.201, f32[1,13,4,1024]{3,0,2,1:T(1,128)S(1)} %copy-done, f32[1,13,12,1024]{3,0,2,1:T(1,128)S(1)} %get-tuple-element.93, ...), kind=kLoop, calls=%fused_computation.54 | loop fusion | flops 1966080 | bytes 5652480 | tf_op jit(solution)/shard_map/sub | solution.py:57
  63.1 4.4 %pad_maximum_fusion.4 = (f32[1,13,16,1024]{3,0,2,1:T(1,128)S(1)}, f32[1,13,16,1024]{3,0,2,1:T(1,128)S(1)}, f32[1,13,16,1024]{3,0,2,1:T(1,128)S(1)}, f32[1,13,16,1024]{3,0,2,1:T(1,128)S(1)}) fusion(f32[1,13,8,1024]{3,0,2,1:T(1,128)S(1)} %get-tuple-element.91, f32[1,11,8,1024]{3,0,2,1:T(1,128)S(1)} %broadcast.367, f32[1,1,8,1024]{3,0,2,1:T(1,128)S(1)} %broadcast.366, ...), kind=kLoop, calls=%fused_computation.22 | loop fusion | flops 1703936 | bytes 5537792 | tf_op jit(solution)/shard_map/concatenate | solution.py:66
  74.4 2.9 %collective-permute-done.6 = f32[1,10,1024]{2,0,1:T(1,128)S(1)} collective-permute-done((f32[1,10,1024]{2,0,1:T(1,128)S(1)}, f32[1,10,1024]{2,0,1:T(1,128)S(1)}, u32[]{:S(2)}, u32[]{:S(2)}) %collective-permute-start.6) | collective-permute-done | bytes 40992 | tf_op jit(solution)/shard_map/ppermute | solution.py:13
  77.4 2.2 %collective-permute-start.7 = (f32[1,11,1024]{2,0,1:T(1,128)S(1)}, f32[1,11,1024]{2,0,1:T(1,128)S(1)}, u32[]{:S(2)}, u32[]{:S(2)}) collective-permute-start(f32[1,11,1024]{2,0,1:T(1,128)S(1)} %pad_maximum_fusion.34), channel_id=1, source_target_pairs={{0,32},{32,64},{64,96},{96,128},{128,160},{160,192},{192,224},{224... | collective-permute-start | bytes 135176 | tf_op jit(solution)/shard_map/ppermute | solution.py:13
  81.9 3.1 %collective-permute-done.8 = f32[1,11,1024]{2,0,1:T(1,128)S(1)} collective-permute-done((f32[1,11,1024]{2,0,1:T(1,128)S(1)}, f32[1,11,1024]{2,0,1:T(1,128)S(1)}, u32[]{:S(2)}, u32[]{:S(2)}) %collective-permute-start.8) | collective-permute-done | bytes 45088 | tf_op jit(solution)/shard_map/ppermute | solution.py:13
  86.6 4.4 %collective-permute-start.9 = (f32[1,11,1024]{2,0,1:T(1,128)S(1)}, f32[1,11,1024]{2,0,1:T(1,128)S(1)}, u32[]{:S(2)}, u32[]{:S(2)}) collective-permute-start(f32[1,11,1024]{2,0,1:T(1,128)S(1)} %pad_maximum_fusion.35), channel_id=1, source_target_pairs={{0,64},{32,96},{64,128},{96,160},{128,192},{160,224},{192,256},{22... | collective-permute-start | bytes 135176 | tf_op jit(solution)/shard_map/ppermute | solution.py:13
  92.4 7.3 %collective-permute-start.11 = (f32[1,11,1024]{2,0,1:T(1,128)S(1)}, f32[1,11,1024]{2,0,1:T(1,128)S(1)}, u32[]{:S(2)}, u32[]{:S(2)}) collective-permute-start(f32[1,11,1024]{2,0,1:T(1,128)S(1)} %pad_maximum_fusion.36), channel_id=1, source_target_pairs={{0,128},{32,160},{64,192},{96,224},{128,256},{160,288},{192,320},{... | collective-permute-start | bytes 135176 | tf_op jit(solution)/shard_map/ppermute | solution.py:13
  101.1 3.1 %collective-permute-start.17 = (f32[1,11,1024]{2,0,1:T(1,128)S(1)}, f32[1,11,1024]{2,0,1:T(1,128)S(1)}, u32[]{:S(2)}, u32[]{:S(2)}) collective-permute-start(f32[1,11,1024]{2,0,1:T(1,128)S(1)} %pad_maximum_fusion.38), channel_id=1, source_target_pairs={{0,32},{32,64},{64,96},{96,128},{128,160},{160,192},{192,224},{224... | collective-permute-start | bytes 135176 | tf_op jit(solution)/shard_map/ppermute | solution.py:13
  106.1 2.9 %collective-permute-done.12 = f32[1,11,1024]{2,0,1:T(1,128)S(1)} collective-permute-done((f32[1,11,1024]{2,0,1:T(1,128)S(1)}, f32[1,11,1024]{2,0,1:T(1,128)S(1)}, u32[]{:S(2)}, u32[]{:S(2)}) %collective-permute-start.12) | collective-permute-done | bytes 45088 | tf_op jit(solution)/shard_map/ppermute | solution.py:13
  109.3 7.6 %collective-permute-start.13 = (f32[1,11,1024]{2,0,1:T(1,128)S(1)}, f32[1,11,1024]{2,0,1:T(1,128)S(1)}, u32[]{:S(2)}, u32[]{:S(2)}) collective-permute-start(f32[1,11,1024]{2,0,1:T(1,128)S(1)} %pad_maximum_fusion.37), channel_id=1, source_target_pairs={{0,256},{32,288},{64,320},{96,352},{128,384},{160,416},{192,448},{... | collective-permute-start | bytes 135176 | tf_op jit(solution)/shard_map/ppermute | solution.py:13
  118.2 7.4 %collective-permute-done.14 = f32[1,11,1024]{2,0,1:T(1,128)S(1)} collective-permute-done((f32[1,11,1024]{2,0,1:T(1,128)S(1)}, f32[1,11,1024]{2,0,1:T(1,128)S(1)}, u32[]{:S(2)}, u32[]{:S(2)}) %collective-permute-start.14) | collective-permute-done | bytes 45088 | tf_op jit(solution)/shard_map/ppermute | solution.py:13
  128.6 3.5 %collective-permute-done.20 = f32[1,11,1024]{2,0,1:T(1,128)S(1)} collective-permute-done((f32[1,11,1024]{2,0,1:T(1,128)S(1)}, f32[1,11,1024]{2,0,1:T(1,128)S(1)}, u32[]{:S(2)}, u32[]{:S(2)}) %collective-permute-start.20) | collective-permute-done | bytes 45088 | tf_op jit(solution)/shard_map/ppermute | solution.py:13
  135.0 9.0 %collective-permute-start.15 = (f32[1,8,1024]{2,0,1:T(1,128)S(1)}, f32[1,8,1024]{2,0,1:T(1,128)S(1)}, u32[]{:S(2)}, u32[]{:S(2)}) collective-permute-start(f32[1,8,1024]{2,0,1:T(1,128)S(1)} %fusion.137), channel_id=1, source_target_pairs={{0,32},{32,64},{64,96},{96,128},{128,160},{160,192},{192,224},{224... | collective-permute-start | bytes 98312 | tf_op jit(solution)/shard_map/ppermute | solution.py:13
  144.3 5.8 %collective-permute-start.23 = (f32[1,11,1024]{2,0,1:T(1,128)S(1)}, f32[1,11,1024]{2,0,1:T(1,128)S(1)}, u32[]{:S(2)}, u32[]{:S(2)}) collective-permute-start(f32[1,11,1024]{2,0,1:T(1,128)S(1)} %pad_maximum_fusion.41), channel_id=1, source_target_pairs={{0,256},{32,288},{64,320},{96,352},{128,384},{160,416},{192,448},{... | collective-permute-start | bytes 135176 | tf_op jit(solution)/shard_map/ppermute | solution.py:13
  151.7 7.7 %collective-permute-done.24 = f32[1,11,1024]{2,0,1:T(1,128)S(1)} collective-permute-done((f32[1,11,1024]{2,0,1:T(1,128)S(1)}, f32[1,11,1024]{2,0,1:T(1,128)S(1)}, u32[]{:S(2)}, u32[]{:S(2)}) %collective-permute-start.24) | collective-permute-done | bytes 45088 | tf_op jit(solution)/shard_map/ppermute | solution.py:13
  159.6 2.8 %collective-permute-start.25 = (f32[1,8,1024]{2,0,1:T(1,128)S(1)}, f32[1,8,1024]{2,0,1:T(1,128)S(1)}, u32[]{:S(2)}, u32[]{:S(2)}) collective-permute-start(f32[1,8,1024]{2,0,1:T(1,128)S(1)} %fusion.138), channel_id=1, source_target_pairs={{0,32},{32,64},{64,96},{96,128},{128,160},{160,192},{192,224},{224... | collective-permute-start | bytes 98312 | tf_op jit(solution)/shard_map/ppermute | solution.py:13
  163.7 4.2 %collective-permute-start.26 = (f32[2,8,1,1024]{3,2,1,0:T(1,128)S(1)}, f32[2,8,1,1024]{3,2,1,0:T(1,128)S(1)}, u32[]{:S(2)}, u32[]{:S(2)}) collective-permute-start(f32[2,8,1,1024]{3,2,1,0:T(1,128)S(1)} %get-tuple-element.87), channel_id=1, source_target_pairs={{0,32},{32,64},{64,96},{96,128},{128,160},{160,192},{192,224},{224... | collective-permute-start | bytes 196616 | tf_op jit(solution)/shard_map/ppermute | solution.py:24
  169.9 3.6 %collective-permute-done.27 = f32[2,8,1,1024]{3,2,1,0:T(1,128)S(1)} collective-permute-done((f32[2,8,1,1024]{3,2,1,0:T(1,128)S(1)}, f32[2,8,1,1024]{3,2,1,0:T(1,128)S(1)}, u32[]{:S(2)}, u32[]{:S(2)}) %collective-permute-start.27) | collective-permute-done | bytes 65568 | tf_op jit(solution)/shard_map/ppermute | solution.py:26
  177.2 6.0 %collective-permute-start.29 = (f32[8,16,1]{2,1,0:T(8,128)S(1)}, f32[8,16,1]{2,1,0:T(8,128)S(1)}, u32[]{:S(2)}, u32[]{:S(2)}) collective-permute-start(f32[8,16,1]{2,1,0:T(8,128)S(1)} %get-tuple-element.111), channel_id=1, source_target_pairs={{1,0},{2,1},{3,2},{4,3},{5,4},{6,5},{7,6},{8,7},{9,8},{10,9},{11,1... | collective-permute-start | bytes 1544 | tf_op jit(solution)/shard_map/ppermute | solution.py:26
  (217 shorter events, 67.1 us)
Async XLA Ops:
  2.4 21.9 %collective-permute-start = (f32[2,1,1024]{2,1,0:T(1,128)S(1)}, f32[2,1,1024]{2,1,0:T(1,128)S(1)}, u32[]{:S(2)}, u32[]{:S(2)}) collective-permute-start(f32[2,1,1024]{2,1,0:T(1,128)S(1)} %get-tuple-element.153), channel_id=1, source_target_pairs={{0,32},{32,64},{64,96},{96,128},{128,160},{160,192},{192,224},{224... | collective-permute-start | bytes 24584 | tf_op jit(solution)/shard_map/ppermute | solution.py:24
  6.2 18.1 %collective-permute-start.1 = (f32[2,1,1024]{2,1,0:T(1,128)S(1)}, f32[2,1,1024]{2,1,0:T(1,128)S(1)}, u32[]{:S(2)}, u32[]{:S(2)}) collective-permute-start(f32[2,1,1024]{2,1,0:T(1,128)S(1)} %get-tuple-element.154), channel_id=1, source_target_pairs={{32,0},{64,32},{96,64},{128,96},{160,128},{192,160},{224,192},{256... | collective-permute-start | bytes 24584 | tf_op jit(solution)/shard_map/ppermute | solution.py:26
  9.1 24.9 %collective-permute-start.4 = (f32[8,16,1]{2,1,0:T(8,128)S(1)}, f32[8,16,1]{2,1,0:T(8,128)S(1)}, u32[]{:S(2)}, u32[]{:S(2)}) collective-permute-start(f32[8,16,1]{2,1,0:T(8,128)S(1)} %get-tuple-element.113), channel_id=1, source_target_pairs={{1,0},{2,1},{3,2},{4,3},{5,4},{6,5},{7,6},{8,7},{9,8},{10,9},{11,1... | collective-permute-start | bytes 1544 | tf_op jit(solution)/shard_map/ppermute | solution.py:26
  20.0 14.0 %collective-permute-start.5 = (f32[8,16,1]{2,1,0:T(8,128)S(1)}, f32[8,16,1]{2,1,0:T(8,128)S(1)}, u32[]{:S(2)}, u32[]{:S(2)}) collective-permute-start(f32[8,16,1]{2,1,0:T(8,128)S(1)} %get-tuple-element.114), channel_id=1, source_target_pairs={{0,1},{1,2},{2,3},{3,4},{4,5},{5,6},{6,7},{7,8},{8,9},{9,10},{10,1... | collective-permute-start | bytes 1544 | tf_op jit(solution)/shard_map/ppermute | solution.py:24
  24.4 7.4 %collective-permute-start.2 = (f32[2,18,1]{2,1,0:T(8,128)S(1)}, f32[2,18,1]{2,1,0:T(8,128)S(1)}, u32[]{:S(2)}, u32[]{:S(2)}) collective-permute-start(f32[2,18,1]{2,1,0:T(8,128)S(1)} %get-tuple-element.146), channel_id=1, source_target_pairs={{0,1},{1,2},{2,3},{3,4},{4,5},{5,6},{6,7},{7,8},{8,9},{9,10},{10,1... | collective-permute-start | bytes 440 | tf_op jit(solution)/shard_map/ppermute | solution.py:24
  26.4 6.4 %collective-permute-start.3 = (f32[2,18,1]{2,1,0:T(8,128)S(1)}, f32[2,18,1]{2,1,0:T(8,128)S(1)}, u32[]{:S(2)}, u32[]{:S(2)}) collective-permute-start(f32[2,18,1]{2,1,0:T(8,128)S(1)} %get-tuple-element.145), channel_id=1, source_target_pairs={{1,0},{2,1},{3,2},{4,3},{5,4},{6,5},{7,6},{8,7},{9,8},{10,9},{11,1... | collective-permute-start | bytes 440 | tf_op jit(solution)/shard_map/ppermute | solution.py:26
  70.5 6.7 %collective-permute-start.6 = (f32[1,10,1024]{2,0,1:T(1,128)S(1)}, f32[1,10,1024]{2,0,1:T(1,128)S(1)}, u32[]{:S(2)}, u32[]{:S(2)}) collective-permute-start(f32[1,10,1024]{2,0,1:T(1,128)S(1)} %slice_bitcast_fusion.7), channel_id=1, source_target_pairs={{32,0},{64,32},{96,64},{128,96},{160,128},{192,160},{224,192},{256... | collective-permute-start | bytes 122888 | tf_op jit(solution)/shard_map/ppermute | solution.py:13
  72.5 9.3 %collective-permute-start.16 = (f32[1,10,1024]{2,0,1:T(1,128)S(1)}, f32[1,10,1024]{2,0,1:T(1,128)S(1)}, u32[]{:S(2)}, u32[]{:S(2)}) collective-permute-start(f32[1,10,1024]{2,0,1:T(1,128)S(1)} %slice_bitcast_fusion.6), channel_id=1, source_target_pairs={{32,0},{64,32},{96,64},{128,96},{160,128},{192,160},{224,192},{256... | collective-permute-start | bytes 122888 | tf_op jit(solution)/shard_map/ppermute | solution.py:13
  85.3 5.7 %collective-permute-start.10 = (f32[1,11,1024]{2,0,1:T(1,128)S(1)}, f32[1,11,1024]{2,0,1:T(1,128)S(1)}, u32[]{:S(2)}, u32[]{:S(2)}) collective-permute-start(f32[1,11,1024]{2,0,1:T(1,128)S(1)} %pad_maximum_fusion.35), channel_id=1, source_target_pairs={{64,0},{96,32},{128,64},{160,96},{192,128},{224,160},{256,192},{28... | collective-permute-start | bytes 135176 | tf_op jit(solution)/shard_map/ppermute | solution.py:13
  92.4 13.7 %collective-permute-start.11 = (f32[1,11,1024]{2,0,1:T(1,128)S(1)}, f32[1,11,1024]{2,0,1:T(1,128)S(1)}, u32[]{:S(2)}, u32[]{:S(2)}) collective-permute-start(f32[1,11,1024]{2,0,1:T(1,128)S(1)} %pad_maximum_fusion.36), channel_id=1, source_target_pairs={{0,128},{32,160},{64,192},{96,224},{128,256},{160,288},{192,320},{... | collective-permute-start | bytes 135176 | tf_op jit(solution)/shard_map/ppermute | solution.py:13
  99.7 9.3 %collective-permute-start.12 = (f32[1,11,1024]{2,0,1:T(1,128)S(1)}, f32[1,11,1024]{2,0,1:T(1,128)S(1)}, u32[]{:S(2)}, u32[]{:S(2)}) collective-permute-start(f32[1,11,1024]{2,0,1:T(1,128)S(1)} %pad_maximum_fusion.36), channel_id=1, source_target_pairs={{128,0},{160,32},{192,64},{224,96},{256,128},{288,160},{320,192},{... | collective-permute-start | bytes 135176 | tf_op jit(solution)/shard_map/ppermute | solution.py:13
  101.1 17.1 %collective-permute-start.17 = (f32[1,11,1024]{2,0,1:T(1,128)S(1)}, f32[1,11,1024]{2,0,1:T(1,128)S(1)}, u32[]{:S(2)}, u32[]{:S(2)}) collective-permute-start(f32[1,11,1024]{2,0,1:T(1,128)S(1)} %pad_maximum_fusion.38), channel_id=1, source_target_pairs={{0,32},{32,64},{64,96},{96,128},{128,160},{160,192},{192,224},{224... | collective-permute-start | bytes 135176 | tf_op jit(solution)/shard_map/ppermute | solution.py:13
  104.2 14.0 %collective-permute-start.18 = (f32[1,11,1024]{2,0,1:T(1,128)S(1)}, f32[1,11,1024]{2,0,1:T(1,128)S(1)}, u32[]{:S(2)}, u32[]{:S(2)}) collective-permute-start(f32[1,11,1024]{2,0,1:T(1,128)S(1)} %pad_maximum_fusion.38), channel_id=1, source_target_pairs={{32,0},{64,32},{96,64},{128,96},{160,128},{192,160},{224,192},{256... | collective-permute-start | bytes 135176 | tf_op jit(solution)/shard_map/ppermute | solution.py:13
  109.3 9.0 %collective-permute-start.13 = (f32[1,11,1024]{2,0,1:T(1,128)S(1)}, f32[1,11,1024]{2,0,1:T(1,128)S(1)}, u32[]{:S(2)}, u32[]{:S(2)}) collective-permute-start(f32[1,11,1024]{2,0,1:T(1,128)S(1)} %pad_maximum_fusion.37), channel_id=1, source_target_pairs={{0,256},{32,288},{64,320},{96,352},{128,384},{160,416},{192,448},{... | collective-permute-start | bytes 135176 | tf_op jit(solution)/shard_map/ppermute | solution.py:13
  116.9 8.7 %collective-permute-start.14 = (f32[1,11,1024]{2,0,1:T(1,128)S(1)}, f32[1,11,1024]{2,0,1:T(1,128)S(1)}, u32[]{:S(2)}, u32[]{:S(2)}) collective-permute-start(f32[1,11,1024]{2,0,1:T(1,128)S(1)} %pad_maximum_fusion.37), channel_id=1, source_target_pairs={{256,0},{288,32},{320,64},{352,96},{384,128},{416,160},{448,192},{... | collective-permute-start | bytes 135176 | tf_op jit(solution)/shard_map/ppermute | solution.py:13
  132.3 11.7 %collective-permute-start.21 = (f32[1,11,1024]{2,0,1:T(1,128)S(1)}, f32[1,11,1024]{2,0,1:T(1,128)S(1)}, u32[]{:S(2)}, u32[]{:S(2)}) collective-permute-start(f32[1,11,1024]{2,0,1:T(1,128)S(1)} %pad_maximum_fusion.40), channel_id=1, source_target_pairs={{0,128},{32,160},{64,192},{96,224},{128,256},{160,288},{192,320},{... | collective-permute-start | bytes 135176 | tf_op jit(solution)/shard_map/ppermute | solution.py:13
  133.7 10.4 %collective-permute-start.22 = (f32[1,11,1024]{2,0,1:T(1,128)S(1)}, f32[1,11,1024]{2,0,1:T(1,128)S(1)}, u32[]{:S(2)}, u32[]{:S(2)}) collective-permute-start(f32[1,11,1024]{2,0,1:T(1,128)S(1)} %pad_maximum_fusion.40), channel_id=1, source_target_pairs={{128,0},{160,32},{192,64},{224,96},{256,128},{288,160},{320,192},{... | collective-permute-start | bytes 135176 | tf_op jit(solution)/shard_map/ppermute | solution.py:13
  135.0 16.6 %collective-permute-start.15 = (f32[1,8,1024]{2,0,1:T(1,128)S(1)}, f32[1,8,1024]{2,0,1:T(1,128)S(1)}, u32[]{:S(2)}, u32[]{:S(2)}) collective-permute-start(f32[1,8,1024]{2,0,1:T(1,128)S(1)} %fusion.137), channel_id=1, source_target_pairs={{0,32},{32,64},{64,96},{96,128},{128,160},{160,192},{192,224},{224... | collective-permute-start | bytes 98312 | tf_op jit(solution)/shard_map/ppermute | solution.py:13
  144.3 7.3 %collective-permute-start.23 = (f32[1,11,1024]{2,0,1:T(1,128)S(1)}, f32[1,11,1024]{2,0,1:T(1,128)S(1)}, u32[]{:S(2)}, u32[]{:S(2)}) collective-permute-start(f32[1,11,1024]{2,0,1:T(1,128)S(1)} %pad_maximum_fusion.41), channel_id=1, source_target_pairs={{0,256},{32,288},{64,320},{96,352},{128,384},{160,416},{192,448},{... | collective-permute-start | bytes 135176 | tf_op jit(solution)/shard_map/ppermute | solution.py:13
  150.2 9.2 %collective-permute-start.24 = (f32[1,11,1024]{2,0,1:T(1,128)S(1)}, f32[1,11,1024]{2,0,1:T(1,128)S(1)}, u32[]{:S(2)}, u32[]{:S(2)}) collective-permute-start(f32[1,11,1024]{2,0,1:T(1,128)S(1)} %pad_maximum_fusion.41), channel_id=1, source_target_pairs={{256,0},{288,32},{320,64},{352,96},{384,128},{416,160},{448,192},{... | collective-permute-start | bytes 135176 | tf_op jit(solution)/shard_map/ppermute | solution.py:13
  163.7 6.2 %collective-permute-start.26 = (f32[2,8,1,1024]{3,2,1,0:T(1,128)S(1)}, f32[2,8,1,1024]{3,2,1,0:T(1,128)S(1)}, u32[]{:S(2)}, u32[]{:S(2)}) collective-permute-start(f32[2,8,1,1024]{3,2,1,0:T(1,128)S(1)} %get-tuple-element.87), channel_id=1, source_target_pairs={{0,32},{32,64},{64,96},{96,128},{128,160},{160,192},{192,224},{224... | collective-permute-start | bytes 196616 | tf_op jit(solution)/shard_map/ppermute | solution.py:24
  167.9 5.6 %collective-permute-start.27 = (f32[2,8,1,1024]{3,2,1,0:T(1,128)S(1)}, f32[2,8,1,1024]{3,2,1,0:T(1,128)S(1)}, u32[]{:S(2)}, u32[]{:S(2)}) collective-permute-start(f32[2,8,1,1024]{3,2,1,0:T(1,128)S(1)} %get-tuple-element.88), channel_id=1, source_target_pairs={{32,0},{64,32},{96,64},{128,96},{160,128},{192,160},{224,192},{256... | collective-permute-start | bytes 196616 | tf_op jit(solution)/shard_map/ppermute | solution.py:26
  175.3 8.0 %collective-permute-start.28 = (f32[8,16,1]{2,1,0:T(8,128)S(1)}, f32[8,16,1]{2,1,0:T(8,128)S(1)}, u32[]{:S(2)}, u32[]{:S(2)}) collective-permute-start(f32[8,16,1]{2,1,0:T(8,128)S(1)} %get-tuple-element.112), channel_id=1, source_target_pairs={{0,1},{1,2},{2,3},{3,4},{4,5},{5,6},{6,7},{7,8},{8,9},{9,10},{10,1... | collective-permute-start | bytes 1544 | tf_op jit(solution)/shard_map/ppermute | solution.py:24
  177.2 7.4 %collective-permute-start.29 = (f32[8,16,1]{2,1,0:T(8,128)S(1)}, f32[8,16,1]{2,1,0:T(8,128)S(1)}, u32[]{:S(2)}, u32[]{:S(2)}) collective-permute-start(f32[8,16,1]{2,1,0:T(8,128)S(1)} %get-tuple-element.111), channel_id=1, source_target_pairs={{1,0},{2,1},{3,2},{4,3},{5,4},{6,5},{7,6},{8,7},{9,8},{10,9},{11,1... | collective-permute-start | bytes 1544 | tf_op jit(solution)/shard_map/ppermute | solution.py:26
  (17 other events, 207.7 us)
where the time goes:
time: 187 us; the launch traced here: 186 us
  starting transfers between devices  101 us (54%)
  waiting for transfers between devices  35.3 us (19%)
  other arithmetic  33.8 us (18%)
  local copies, waits for them, and re-layouts  14.3 us (8%)
  between operations  2.11 us (1%)
    ppermute x20, starting transfers between devices, shifted(): return lax.ppermute(x, axis, pairs)  60.5 us
    ppermute x20, waiting for transfers between devices, shifted(): return lax.ppermute(x, axis, pairs)  29.4 us
    ppermute x5, starting transfers between devices, padded(): lax.ppermute(head, axis, [((i + 1) % count, i) for i in range(ends)])  26.3 us
    ppermute x5, starting transfers between devices, padded(): lax.ppermute(tail, axis, [(i, (i + 1) % count) for i in range(ends)])  13.7 us
    sub x10, other arithmetic, reduce_level(): current[:, 3:] - left_factor * lower_rows[:, 3:]  9.98 us
    slice x8, local copies, waits for them, and re-layouts, local_sweep(): packed[:, :, :length - stride]  7.37 us
    ppermute x5, waiting for transfers between devices, padded(): lax.ppermute(head, axis, [((i + 1) % count, i) for i in range(ends)])  5.86 us
    concatenate x12, other arithmetic, reduce_level(): return jnp.concatenate([new_lower, new_middle, new_upper, new_rhs], axis=1)  5.45 us
  transfers between devices with their start and end apart: 30, of which 11 were waited for; matrix products, arithmetic and copies ran while one was open for 3% of the time, Pallas kernels for 0%

commit v1 on v0

v1 whole, which is shorter than its diff:
```python
import functools

import jax
import jax.numpy as jnp
from jax import lax
from jax.experimental import pallas as pl
from jax.experimental.pallas import tpu as pltpu
from jax.sharding import PartitionSpec as P

implicit_ratio = 4000.0
explicit_ratio = 0.1
LANES = 128
SUBLANES = 8


def spread_columns(lane, pieces):
    out = jnp.zeros(lane.shape, jnp.float32)
    for low, count, column in pieces:
        out = jnp.where((lane >= low) & (lane < low + count), column, out)
    return out


def edge_kernel(rows, tests, hb0, hb1, seed0, seed1, logk0, logk1, mask0, mask1, to_right, to_left, own):
    lane = lax.broadcasted_iota(jnp.int32, (rows, LANES), 1)
    sides = []
    for hb, seed, logk, mask, c in ((hb0, seed0, logk0, mask0, 0), (hb1, seed1, logk1, mask1, LANES - 1)):
        conduct = jnp.exp(logk[:, c : c + 1])
        active = (1 - mask[:, c : c + 1]).astype(jnp.float32)
        heads = [hb[rows * t : rows * (t + 1), c : c + 1] for t in range(tests)]
        seeds = [active * seed[rows * t : rows * (t + 1), c : c + 1] for t in range(tests)]
        sides.append((conduct, active, heads, seeds))

    def packed(side, odd, with_seed):
        conduct, active, heads, seeds = sides[side]
        base = tests * odd
        pieces = [(2 * tests + base + t, 1, heads[t]) for t in range(tests)]
        pieces += [(4 * tests + base, tests, conduct), (6 * tests + base, tests, active)]
        if with_seed:
            pieces += [(base + t, 1, seeds[t]) for t in range(tests)]
        return spread_columns(lane, pieces)

    to_right[...] = packed(1, 0, True)
    to_left[...] = packed(0, 1, True)
    own[...] = packed(0, 0, False) + packed(1, 1, False)


def eliminate(conduct, active):
    rows = len(conduct)
    gains, inverses, backs = [None], [], []
    excess = jnp.ones_like(conduct[0])
    face = None
    for i in range(rows):
        if i > 0:
            gain = active[i] * face * inverses[-1]
            gains.append(gain)
            excess = 1.0 + gain * excess
        if i < rows - 1:
            face = (2.0 * implicit_ratio) * conduct[i] * conduct[i + 1] / (conduct[i] + conduct[i + 1])
            upper = active[i] * face
            inverse = 1.0 / (excess + upper)
            backs.append(upper * inverse)
        else:
            inverse = 1.0 / excess
            backs.append(None)
        inverses.append(inverse)
    return gains, inverses, backs


def sweep(gains, inverses, backs, right):
    rows = len(right)
    held = [right[0]]
    for i in range(1, rows):
        held.append(right[i] + gains[i] * held[-1])
    values = [None] * rows
    values[-1] = held[-1] * inverses[-1]
    for i in range(rows - 2, -1, -1):
        values[i] = held[i] * inverses[i] + backs[i] * values[i + 1]
    return values


def responses(gains, inverses, backs, active):
    rows = len(active)
    held = [active[0]]
    for i in range(1, rows):
        held.append(gains[i] * held[-1])
    first, last = [None] * rows, [None] * rows
    first[-1] = held[-1] * inverses[-1]
    last[-1] = active[-1] * inverses[-1]
    for i in range(rows - 2, -1, -1):
        first[i] = held[i] * inverses[i] + backs[i] * first[i + 1]
        last[i] = backs[i] * last[i + 1]
    return first, last


def local_kernel(
    rows, tests, total_columns, wells, rates, hb, seed, logk, mask, from_left, from_right, own,
    message, heads_part, adjoint_part, first_out, last_out, side_part, side_first, side_last,
    right, weighed, cond_c, act_c, gain_c, inv_c, back_c, first_c, last_c,
):
    columns = hb.shape[1]
    tiles = columns // LANES
    field = tests * rows
    conduct = jnp.exp(logk[...])
    active = (1 - mask[...]).astype(jnp.float32)
    for k in range(tiles):
        cond_c[pl.ds(k, rows, stride=tiles), :] = conduct[:, k * LANES : (k + 1) * LANES]
        act_c[pl.ds(k, rows, stride=tiles), :] = active[:, k * LANES : (k + 1) * LANES]
    cond_rows = [cond_c[tiles * i : tiles * (i + 1), :] for i in range(rows)]
    act_rows = [act_c[tiles * i : tiles * (i + 1), :] for i in range(rows)]
    gains, inverses, backs = eliminate(cond_rows, act_rows)
    first, last = responses(gains, inverses, backs, act_rows)
    for i in range(rows):
        here = slice(tiles * i, tiles * (i + 1))
        if i > 0:
            gain_c[here, :] = gains[i]
        inv_c[here, :] = inverses[i]
        if i < rows - 1:
            back_c[here, :] = backs[i]
        first_c[here, :] = first[i]
        last_c[here, :] = last[i]
    half = 0.5 / implicit_ratio
    first_end = first[0] + half / cond_rows[0]
    last_end = last[-1] + half / cond_rows[-1]
    across = first[-1]

    lane = lax.broadcasted_iota(jnp.int32, (rows, columns), 1)
    cond_north = pltpu.roll(conduct, columns - 1, 1)
    face = (2.0 * explicit_ratio) * conduct * cond_north / (conduct + cond_north)
    face = jnp.where(lane == columns - 1, 0.0, face)
    for t in range(tests):
        here = slice(rows * t, rows * (t + 1))
        head = hb[here, :]
        flow = face * (pltpu.roll(head, columns - 1, 1) - head)
        value = head + active * (flow - pltpu.roll(flow, 1, 1))
        seeded = active * seed[here, :]
        for k in range(tiles):
            lanes = slice(k * LANES, (k + 1) * LANES)
            there = slice(k * field + rows * t, k * field + rows * (t + 1))
            right[there, :] = value[:, lanes]
            weighed[there, :] = seeded[:, lanes]
    row_start = lax.axis_index("gx") * rows
    column_start = lax.axis_index("gy") * columns
    row_lane = lax.broadcasted_iota(jnp.int32, (1, LANES), 1)
    for t in range(tests):
        well = wells[t]
        well_row = well // total_columns - row_start
        well_column = well % total_columns - column_start
        inside = (well_row >= 0) & (well_row < rows) & (well_column >= 0) & (well_column < columns)

        @pl.when(inside)
        def _():
            tile = well_column // LANES
            act_row = act_c[pl.ds(tiles * well_row + tile, 1), :]
            there = pl.ds(tile * field + rows * t + well_row, 1)
            added = jnp.where(row_lane == well_column % LANES, act_row * rates[t], 0.0)
            right[there, :] = right[there, :] + added

    for k in range(tiles):
        lanes = slice(k * LANES, (k + 1) * LANES)
        gain_k = [None] + [gain_c[tiles * i + k : tiles * i + k + 1, :] for i in range(1, rows)]
        inv_k = [inv_c[tiles * i + k : tiles * i + k + 1, :] for i in range(rows)]
        back_k = [back_c[tiles * i + k : tiles * i + k + 1, :] for i in range(rows - 1)] + [None]
        for core, (source, out) in enumerate(((right, heads_part), (weighed, adjoint_part))):
            given = [source[pl.ds(k * field + i, tests, stride=rows), :] for i in range(rows)]
            values = sweep(gain_k, inv_k, back_k, given)
            for i in range(rows):
                out[pl.ds(k * field + i, tests, stride=rows), :] = values[i]
            dest = 2 * k + core
            message[dest, 0:tests, :] = values[0]
            message[dest, tests : 2 * tests, :] = values[-1]
            message[dest, 16:17, :] = first_end[k : k + 1, :]
            message[dest, 17:18, :] = last_end[k : k + 1, :]
            message[dest, 18:19, :] = across[k : k + 1, :]
        first_out[:, lanes] = first_c[pl.ds(k, rows, stride=tiles), :]
        last_out[:, lanes] = last_c[pl.ds(k, rows, stride=tiles), :]

    halo = from_left[...] + from_right[...]
    mine = own[...]
    side_lane = lax.broadcasted_iota(jnp.int32, (rows, LANES), 1)
    outer = side_lane < 2 * tests
    halo_k = pltpu.roll(halo, LANES - 2 * tests, 1)
    own_k = pltpu.roll(mine, LANES - 2 * tests, 1)
    cond_s = jnp.where(outer, pltpu.roll(halo, LANES - 4 * tests, 1), own_k)
    cond_s = jnp.where(cond_s > 0.0, cond_s, 1.0)
    act_s = jnp.where(outer, pltpu.roll(halo, LANES - 6 * tests, 1), pltpu.roll(mine, LANES - 4 * tests, 1))
    side_face = (2.0 * explicit_ratio) * cond_s * halo_k / (cond_s + halo_k)
    given_s = jnp.where(outer, halo, act_s * side_face * (halo - mine))
    cond_sr = [cond_s[i : i + 1, :] for i in range(rows)]
    act_sr = [act_s[i : i + 1, :] for i in range(rows)]
    gains_s, inv_s, backs_s = eliminate(cond_sr, act_sr)
    first_s, last_s = responses(gains_s, inv_s, backs_s, act_sr)
    part_s = sweep(gains_s, inv_s, backs_s, [given_s[i : i + 1, :] for i in range(rows)])
    for i in range(rows):
        side_part[i : i + 1, :] = part_s[i]
        side_first[i : i + 1, :] = first_s[i]
        side_last[i : i + 1, :] = last_s[i]
    ends = (
        part_s[0], part_s[-1], first_s[0] + half / cond_sr[0], last_s[-1] + half / cond_sr[-1], first_s[-1],
    )
    for dest in range(2 * tiles):
        for r, value in enumerate(ends):
            message[dest, 19 + r : 20 + r, :] = value


def chain(first_end, last_end, across, first_value, last_value):
    count = len(first_end)
    diag = [None] + [last_end[i - 1] + first_end[i] for i in range(1, count)]
    load = [None] + [last_value[i - 1] - first_value[i] for i in range(1, count)]
    middle = count // 2
    inverse = [None] * count
    for i in range(1, middle):
        if i > 1:
            factor = across[i - 1] * inverse[i - 1]
            diag[i] = diag[i] - factor * across[i - 1]
            load[i] = load[i] + factor * load[i - 1]
        inverse[i] = 1.0 / diag[i]
    for i in range(count - 1, middle, -1):
        if i < count - 1:
            factor = across[i] * inverse[i + 1]
            diag[i] = diag[i] - factor * across[i]
            load[i] = load[i] + factor * load[i + 1]
        inverse[i] = 1.0 / diag[i]
    below = across[middle - 1] * inverse[middle - 1]
    above = across[middle] * inverse[middle + 1]
    diag[middle] = diag[middle] - below * across[middle - 1] - above * across[middle]
    load[middle] = load[middle] + below * load[middle - 1] + above * load[middle + 1]
    flux = [None] * count
    flux[middle] = load[middle] / diag[middle]
    for i in range(middle - 1, 0, -1):
        flux[i] = (load[i] + across[i] * flux[i + 1]) * inverse[i]
    for i in range(middle + 1, count):
        flux[i] = (load[i] + across[i - 1] * flux[i - 1]) * inverse[i]
    nothing = jnp.zeros_like(flux[middle])
    return [nothing] + flux[1:] + [nothing]


def line_kernel(devices, tests, got, reply, side_flux, held):
    def solve(first_end, last_end, across, first_value, last_value):
        def pick(span):
            return [got[d, span, :] for d in range(devices)]

        return chain(pick(first_end), pick(last_end), pick(across), pick(first_value), pick(last_value))

    side = solve(slice(21, 22), slice(22, 23), slice(23, 24), slice(19, 20), slice(20, 21))
    for d in range(devices + 1):
        held[d : d + 1, :] = side[d]
    flux = solve(slice(16, 17), slice(17, 18), slice(18, 19), slice(0, tests), slice(tests, 2 * tests))
    for d in range(devices):
        reply[d, 0:tests, :] = flux[d]
        reply[d, tests : 2 * tests, :] = flux[d + 1]
    me = lax.axis_index("gx")
    side_flux[0:1, :] = held[pl.ds(me, 1), :]
    side_flux[1:2, :] = held[pl.ds(me + 1, 1), :]


def final_kernel(
    rows, tests, hb, logk, heads_part, adjoint_part, first_in, last_in, got, from_left, from_right,
    side_part, side_first, side_last, side_flux, heads, sensitivity,
):
    columns = hb.shape[1]
    tiles = columns // LANES
    side = side_part[...] + side_first[...] * side_flux[0:1, :] - side_last[...] * side_flux[1:2, :]
    halo = from_left[...] + from_right[...]
    conduct = jnp.exp(logk[...])
    first = first_in[...]
    last = last_in[...]
    lane = lax.broadcasted_iota(jnp.int32, (rows, columns), 1)
    row = lax.broadcasted_iota(jnp.int32, (rows, columns), 0)
    at_start = lane == 0
    at_end = lane == columns - 1

    def wide(core, r):
        return jnp.concatenate([got[2 * k + core, r : r + 1, :] for k in range(tiles)], axis=1)

    def joined(part, t):
        starts = [(k * tests + t) * rows for k in range(tiles)]
        return jnp.concatenate([part[start : start + rows, :] for start in starts], axis=1)

    def beside(values, index):
        return values[:, index : index + 1]

    row_lane = lax.broadcasted_iota(jnp.int32, (1, columns), 1)
    end_products = [jnp.zeros((1, columns), jnp.float32)] * 2
    along_rows = jnp.zeros((rows, columns), jnp.float32)
    along_columns = jnp.zeros((rows, columns), jnp.float32)
    start_face = jnp.zeros((rows, LANES), jnp.float32)
    for t in range(tests):
        here = slice(rows * t, rows * (t + 1))
        fluxes = [[wide(core, base + t) for base in (0, tests)] for core in (0, 1)]
        head = joined(heads_part, t) + first * fluxes[0][0] - last * fluxes[0][1]
        head = head + jnp.where(at_start, beside(side, 2 * tests + t), 0.0)
        head = head + jnp.where(at_end, beside(side, 3 * tests + t), 0.0)
        heads[here, :] = head
        weight = joined(adjoint_part, t) + first * fluxes[1][0] - last * fluxes[1][1]
        for end in (0, 1):
            side_row = side_flux[end : end + 1, :]
            whole = fluxes[0][end] + jnp.where(row_lane == 0, beside(side_row, 2 * tests + t), 0.0)
            whole = whole + jnp.where(row_lane == columns - 1, beside(side_row, 3 * tests + t), 0.0)
            end_products[end] = end_products[end] + whole * fluxes[1][end]
        east_head = pltpu.roll(head, rows - 1, 0)
        east_weight = pltpu.roll(weight, rows - 1, 0)
        along_rows = along_rows + (east_head - head) * (weight - east_weight)
        old = hb[here, :]
        north_old = jnp.where(at_end, beside(halo, 3 * tests + t), pltpu.roll(old, columns - 1, 1))
        north_weight = jnp.where(at_end, beside(side, tests + t), pltpu.roll(weight, columns - 1, 1))
        along_columns = along_columns + (north_old - old) * (weight - north_weight)
        start_face = start_face + (old[:, :LANES] - beside(halo, 2 * tests + t)) * (
            beside(side, t) - weight[:, :LANES]
        )
    cond_east = pltpu.roll(conduct, rows - 1, 0)
    face = 2.0 * conduct * cond_east / (conduct + cond_east)
    face = jnp.where(row == rows - 1, 0.0, face)
    share = implicit_ratio * face * face * along_rows
    total = share + pltpu.roll(share, 1, 0)
    cond_north = jnp.where(at_end, beside(halo, 5 * tests), pltpu.roll(conduct, columns - 1, 1))
    face = 2.0 * conduct * cond_north / (conduct + cond_north)
    share = explicit_ratio * face * face * along_columns
    cond_start = conduct[:, :LANES]
    cond_south = jnp.broadcast_to(beside(halo, 4 * tests), (rows, LANES))
    face = 2.0 * cond_start * cond_south / (cond_start + cond_south)
    start_share = explicit_ratio * face * face * start_face
    start_share = jnp.concatenate([start_share, jnp.zeros((rows, columns - LANES), jnp.float32)], axis=1)
    total = total + share + jnp.where(at_start, start_share, pltpu.roll(share, 1, 1))
    scale = -1.0 / implicit_ratio
    total = total + jnp.where(row == 0, scale * end_products[0], 0.0)
    total = total + jnp.where(row == rows - 1, scale * end_products[1], 0.0)
    sensitivity[...] = total * (0.5 / conduct)


def f32(*shape):
    return jax.ShapeDtypeStruct(shape, jnp.float32)


VMEM = pl.BlockSpec(memory_space=pltpu.VMEM)
SMEM = pl.BlockSpec(memory_space=pltpu.SMEM)
PARAMS = pltpu.CompilerParams(vmem_limit_bytes=40 * 1024 * 1024)


def per_device(head_before, log_conductivity, fixed_mask, well_cells, pump_rates, adjoint_seed):
    tests, rows, columns = head_before.shape
    tiles = columns // LANES
    devices = lax.axis_size("gx")
    peers = lax.axis_size("gy")
    hb = head_before.reshape(tests * rows, columns)
    seed = adjoint_seed.reshape(tests * rows, columns)

    def ends(height):
        return [pl.BlockSpec((height, LANES), lambda i, k=k: (0, k)) for k in (0, tiles - 1)]

    small = pl.BlockSpec((rows, LANES), lambda i: (0, 0))
    to_right, to_left, own = pl.pallas_call(
        functools.partial(edge_kernel, rows, tests),
        grid=(1,),
        in_specs=ends(tests * rows) * 2 + ends(rows) * 2,
        out_specs=[small] * 3,
        out_shape=[f32(rows, LANES)] * 3,
        compiler_params=PARAMS,
        name="edges",
    )(hb, hb, seed, seed, log_conductivity, log_conductivity, fixed_mask, fixed_mask)
    from_left = lax.ppermute(to_right, "gy", [(i, i + 1) for i in range(peers - 1)])
    from_right = lax.ppermute(to_left, "gy", [(i + 1, i) for i in range(peers - 1)])

    part = f32(tiles * tests * rows, LANES)
    message, heads_part, adjoint_part, first, last, side_part, side_first, side_last = pl.pallas_call(
        functools.partial(local_kernel, rows, tests, columns * peers),
        in_specs=[SMEM] * 2 + [VMEM] * 7,
        out_specs=[VMEM] * 8,
        out_shape=[f32(devices, 24, LANES), part, part] + [f32(rows, columns)] * 2 + [f32(rows, LANES)] * 3,
        scratch_shapes=[pltpu.VMEM((tiles * tests * rows, LANES), jnp.float32)] * 2
        + [pltpu.VMEM((rows * tiles, LANES), jnp.float32)] * 7,
        compiler_params=PARAMS,
        name="local",
    )(well_cells, pump_rates, hb, seed, log_conductivity, fixed_mask, from_left, from_right, own)
    got = lax.all_to_all(message, "gx", 0, 0)
    reply, side_flux = pl.pallas_call(
        functools.partial(line_kernel, devices, tests),
        in_specs=[VMEM],
        out_specs=[VMEM] * 2,
        out_shape=[f32(devices, 2 * tests, LANES), f32(SUBLANES, LANES)],
        scratch_shapes=[pltpu.VMEM((devices + SUBLANES, LANES), jnp.float32)],
        compiler_params=PARAMS,
        name="line",
    )(got)
    answer = lax.all_to_all(reply, "gx", 0, 0)
    heads, sensitivity = pl.pallas_call(
        functools.partial(final_kernel, rows, tests),
        in_specs=[VMEM] * 13,
        out_specs=[VMEM] * 2,
        out_shape=[f32(tests * rows, columns), f32(rows, columns)],
        compiler_params=PARAMS,
        name="final",
    )(
        hb, log_conductivity, heads_part, adjoint_part, first, last, answer, from_left, from_right,
        side_part, side_first, side_last, side_flux,
    )
    return heads.reshape(tests, rows, columns), sensitivity


def solution(mesh):
    return jax.shard_map(
        per_device,
        mesh=mesh,
        in_specs=(P(None, "gx", "gy"), P("gx", "gy"), P("gx", "gy"), P(), P(), P(None, "gx", "gy")),
        out_specs=(P(None, "gx", "gy"), P("gx", "gy")),
        check_vma=False,
    )
```

time: 187 us -> 53.4 us (0.29)
  starting transfers between devices: 101 us -> 12.9 us
  waiting for transfers between devices: 35.3 us -> 0.76 us
  other arithmetic: 33.8 us -> 0 us
  blocking collectives: 0 us -> 30.9 us
  local copies, waits for them, and re-layouts: 14.3 us -> 3.78 us
  Pallas kernels: 0 us -> 4.03 us
    ppermute x30 -> x2, starting transfers between devices: 101 us -> 12.9 us  [the longest x1 8.85 us: per_device(): lax.ppermute(to_left, 'gy', [(i + 1, i) for i in range(peers - 1)])]
    ppermute x30 -> x2, waiting for transfers between devices: 35.3 us -> 0.76 us  [the longest x1 0.76 us: per_device(): lax.ppermute(to_left, 'gy', [(i + 1, i) for i in range(peers - 1)])]
    all_to_all x0 -> x2, blocking collectives: none -> 30.9 us  [the longest x1 18.9 us: per_device(): got = lax.all_to_all(message, 'gx', 0, 0)]
    sub x28 -> x0, other arithmetic: 12.7 us -> none  [the longest x10 9.98 us: reduce_level(): current[:, 3:] - left_factor * lower_rows[:, 3:]]
    concatenate x18 -> x0, other arithmetic: 10.5 us -> none  [the longest x12 5.45 us: reduce_level(): return jnp.concatenate([new_lower, new_middle, new_upper, new_rhs], axis=1)]
    slice x16 -> x0, local copies, waits for them, and re-layouts: 8.54 us -> none  [the longest x8 7.37 us: local_sweep(): packed[:, :, :length - stride]]
    pallas_call x0 -> x4, Pallas kernels: none -> 4.03 us  [the longest x1 2.2 us: per_device(): pl.pallas_call(functools.partial(local_kernel, rows, tests, columns * pee...]
    unnamed x44 -> x16, local copies, waits for them, and re-layouts: 0.57 us -> 3.78 us
  transfers between devices with their start and end apart: 30 -> 2, of which waited for: 11 -> 1; matrix products, arithmetic and copies ran while one was open for 3% -> 0% of each run, Pallas kernels for 0% -> 0%
where the time goes in v1:
time: 53.4 us; the launch traced here: 53 us
  blocking collectives  30.9 us (58%)
  starting transfers between devices  12.9 us (24%)
  Pallas kernels  4.03 us (8%)
  local copies, waits for them, and re-layouts  3.78 us (7%)
  waiting for transfers between devices  0.76 us (1%)
  between operations  0.72 us (1%)
    all_to_all x1, blocking collectives, per_device(): got = lax.all_to_all(message, 'gx', 0, 0)  18.9 us
    all_to_all x1, blocking collectives, per_device(): answer = lax.all_to_all(reply, 'gx', 0, 0)  12 us
    ppermute x1, starting transfers between devices, per_device(): lax.ppermute(to_left, 'gy', [(i + 1, i) for i in range(peers - 1)])  8.85 us
    ppermute x1, starting transfers between devices, per_device(): lax.ppermute(to_right, 'gy', [(i, i + 1) for i in range(peers - 1)])  4 us
    unnamed x16, local copies, waits for them, and re-layouts  3.78 us
    pallas_call x1, Pallas kernels, per_device(): pl.pallas_call(functools.partial(local_kernel, rows, tests, columns * pee...  2.2 us
    pallas_call x1, Pallas kernels, per_device(): pl.pallas_call(functools.partial(final_kernel, rows, tests), in_specs=[VM...  1.59 us
  transfers between devices with their start and end apart: 2, of which 1 were waited for; matrix products, arithmetic and copies ran while one was open for 0% of the time, Pallas kernels for 0%

profile of v1, /device:TPU:7, one launch (start us, length us, event | category | flops | bytes accessed | tf_op | source)
XLA Modules:
  0.0 53.0 jit_solution(6884452583317314435)
XLA Ops:
  0.6 0.0 copy-start
  0.6 1.0 %copy-done = f32[8,16,1024]{2,1,0:T(8,128)S(1)} copy-done((f32[8,16,1024]{2,1,0:T(8,128)S(1)}, f32[8,16,1024]{2,1,0:T(8,128)}, u32[]{:S(2)}) %copy-start) | copy-done | bytes 524312
  1.7 0.0 copy-start.2
  1.7 1.0 %copy-done.2 = f32[8,16,1024]{2,1,0:T(8,128)S(1)} copy-done((f32[8,16,1024]{2,1,0:T(8,128)S(1)}, f32[8,16,1024]{2,1,0:T(8,128)}, u32[]{:S(2)}) %copy-start.2) | copy-done | bytes 524312
  2.7 0.8 %copy-done.3 = f32[16,1024]{1,0:T(8,128)S(1)} copy-done((f32[16,1024]{1,0:T(8,128)S(1)}, f32[16,1024]{1,0:T(8,128)}, u32[]{:S(2)}) %copy-start.3) | copy-done | bytes 65560
  3.6 0.8 %copy-done.5 = s32[16,1024]{1,0:T(8,128)S(1)} copy-done((s32[16,1024]{1,0:T(8,128)S(1)}, s32[16,1024]{1,0:T(8,128)}, u32[]{:S(2)}) %copy-start.5) | copy-done | bytes 65560
  4.4 0.1 edges.1
  4.5 4.0 %collective-permute-start = (f32[16,128]{1,0:T(8,128)S(1)}, f32[16,128]{1,0:T(8,128)S(1)}, u32[]{:S(2)}, u32[]{:S(2)}) collective-permute-start(f32[16,128]{1,0:T(8,128)S(1)} %get-tuple-element.17), channel_id=1, source_target_pairs={{0,1},{1,2},{2,3},{3,4},{4,5},{5,6},{6,7},{7,8},{8,9},{9,10},{10,1... | collective-permute-start | bytes 24584 | tf_op jit(solution)/shard_map/ppermute | solution.py:360
  8.6 0.0 copy-start.6
  8.6 0.0 copy-start.7
  8.6 8.9 %collective-permute-start.1 = (f32[16,128]{1,0:T(8,128)S(1)}, f32[16,128]{1,0:T(8,128)S(1)}, u32[]{:S(2)}, u32[]{:S(2)}) collective-permute-start(f32[16,128]{1,0:T(8,128)S(1)} %get-tuple-element.18), channel_id=1, source_target_pairs={{1,0},{2,1},{3,2},{4,3},{5,4},{6,5},{7,6},{8,7},{9,8},{10,9},{11,1... | collective-permute-start | bytes 24584 | tf_op jit(solution)/shard_map/ppermute | solution.py:361
  17.4 0.0 collective-permute-done.from_left
  17.4 0.8 %collective-permute-done.1.from_right = f32[16,128]{1,0:T(8,128)S(1)} collective-permute-done((f32[16,128]{1,0:T(8,128)S(1)}, f32[16,128]{1,0:T(8,128)S(1)}, u32[]{:S(2)}, u32[]{:S(2)}) %collective-permute-start.1) | collective-permute-done | bytes 8224 | tf_op jit(solution)/shard_map/ppermute | solution.py:361
  18.2 0.0 copy-done.6
  18.2 0.0 copy-done.7
  18.2 2.2 %local.1 = (f32[16,24,128]{2,1,0:T(8,128)S(1)}, f32[1024,128]{1,0:T(8,128)S(1)}, f32[1024,128]{1,0:T(8,128)S(1)}, f32[16,1024]{1,0:T(8,128)S(1)}, f32[16,1024]{1...) custom-call(s32[8]{0:T(128)S(1)} %copy-done.6, f32[8]{0:T(128)S(1)} %copy-done.7, ...), custom_call_target="tpu_custom_call" | custom-call | tf_op jit(solution)/shard_map/local/pallas_call | solution.py:364
  20.4 0.0 copy-start.1
  20.4 18.9 %all_to_all.10.got = f32[16,24,128]{2,1,0:T(8,128)S(1)} all-to-all(f32[16,24,128]{2,1,0:T(8,128)S(1)} %get-tuple-element.24), channel_id=1, replica_groups=mesh['gx'=16,'gy'=32] {'gx'}, dimensions={0} | all-to-all | bytes 393216 | tf_op jit(solution)/shard_map/all_to_all | solution.py:374
  39.3 0.1 line.1
  39.4 0.0 copy-start.4
  39.4 12.0 %all_to_all.11.got = f32[16,16,128]{2,1,0:T(8,128)S(1)} all-to-all(f32[16,16,128]{2,1,0:T(8,128)S(1)} %get-tuple-element.25), channel_id=1, replica_groups=mesh['gx'=16,'gy'=32] {'gx'}, dimensions={0} | all-to-all | bytes 262144 | tf_op jit(solution)/shard_map/all_to_all | solution.py:384
  51.4 0.0 copy-done.1
  51.4 0.0 copy-done.4
  51.4 1.6 %final.1 = (f32[128,1024]{1,0:T(8,128)}, f32[16,1024]{1,0:T(8,128)}) custom-call(f32[128,1024]{1,0:T(8,128)S(1)} %bitcast.6, f32[16,1024]{1,0:T(8,128)S(1)} %copy-done.4, f32[1024,128]{1,0:T(8,128)S(1)} %get-tuple-element.20.heads_part, f32[1024,128]{1,0:T(8,128)S(1)} %get-tuple-element.21.adjoint_part, f32[16,1024]{1,0:T(8,128)S(1)} %get-tuple-element.22.first_in, ...), custom_call_target="tpu_custom_call" | custom-call | tf_op jit(solution)/shard_map/final/pallas_call | solution.py:385
  (2 shorter events, 0.0 us)
Async XLA Ops:
  0.6 1.0 %copy-start = (f32[8,16,1024]{2,1,0:T(8,128)S(1)}, f32[8,16,1024]{2,1,0:T(8,128)}, u32[]{:S(2)}) copy-start(f32[8,16,1024]{2,1,0:T(8,128)} %param.6) | copy-start | bytes 1572868
  1.7 1.0 %copy-start.2 = (f32[8,16,1024]{2,1,0:T(8,128)S(1)}, f32[8,16,1024]{2,1,0:T(8,128)}, u32[]{:S(2)}) copy-start(f32[8,16,1024]{2,1,0:T(8,128)} %param.11) | copy-start | bytes 1572868
  2.7 0.8 %copy-start.3 = (f32[16,1024]{1,0:T(8,128)S(1)}, f32[16,1024]{1,0:T(8,128)}, u32[]{:S(2)}) copy-start(f32[16,1024]{1,0:T(8,128)} %logk.3) | copy-start | bytes 196612
  3.6 0.8 %copy-start.5 = (s32[16,1024]{1,0:T(8,128)S(1)}, s32[16,1024]{1,0:T(8,128)}, u32[]{:S(2)}) copy-start(s32[16,1024]{1,0:T(8,128)} %mask.1) | copy-start | bytes 196612
  4.5 12.9 %collective-permute-start = (f32[16,128]{1,0:T(8,128)S(1)}, f32[16,128]{1,0:T(8,128)S(1)}, u32[]{:S(2)}, u32[]{:S(2)}) collective-permute-start(f32[16,128]{1,0:T(8,128)S(1)} %get-tuple-element.17), channel_id=1, source_target_pairs={{0,1},{1,2},{2,3},{3,4},{4,5},{5,6},{6,7},{7,8},{8,9},{9,10},{10,1... | collective-permute-start | bytes 24584 | tf_op jit(solution)/shard_map/ppermute | solution.py:360
  8.6 9.7 %copy-start.6 = (s32[8]{0:T(128)S(1)}, s32[8]{0:T(128)}, u32[]{:S(2)}) copy-start(s32[8]{0:T(128)} %wells.1) | copy-start | bytes 100
  8.6 9.6 %copy-start.7 = (f32[8]{0:T(128)S(1)}, f32[8]{0:T(128)}, u32[]{:S(2)}) copy-start(f32[8]{0:T(128)} %rates.1) | copy-start | bytes 100
  8.6 9.6 %collective-permute-start.1 = (f32[16,128]{1,0:T(8,128)S(1)}, f32[16,128]{1,0:T(8,128)S(1)}, u32[]{:S(2)}, u32[]{:S(2)}) collective-permute-start(f32[16,128]{1,0:T(8,128)S(1)} %get-tuple-element.18), channel_id=1, source_target_pairs={{1,0},{2,1},{3,2},{4,3},{5,4},{6,5},{7,6},{8,7},{9,8},{10,9},{11,1... | collective-permute-start | bytes 24584 | tf_op jit(solution)/shard_map/ppermute | solution.py:361
  20.4 31.0 %copy-start.1 = (f32[8,16,1024]{2,1,0:T(8,128)S(1)}, f32[8,16,1024]{2,1,0:T(8,128)}, u32[]{:S(2)}) copy-start(f32[8,16,1024]{2,1,0:T(8,128)} %param.6) | copy-start | bytes 1572868
  39.4 12.0 %copy-start.4 = (f32[16,1024]{1,0:T(8,128)S(1)}, f32[16,1024]{1,0:T(8,128)}, u32[]{:S(2)}) copy-start(f32[16,1024]{1,0:T(8,128)} %logk.3) | copy-start | bytes 196612

commit v2 on v1

--- a/solution.py
+++ b/solution.py
@@ -20,15 +20,15 @@
     return out
 
 
-def edge_kernel(rows, tests, hb0, hb1, seed0, seed1, logk0, logk1, mask0, mask1, to_right, to_left, own):
+def edge_messages(rows, tests, hb, seed, conduct, active, to_right, to_left, own):
+    columns = hb.shape[1]
     lane = lax.broadcasted_iota(jnp.int32, (rows, LANES), 1)
     sides = []
-    for hb, seed, logk, mask, c in ((hb0, seed0, logk0, mask0, 0), (hb1, seed1, logk1, mask1, LANES - 1)):
-        conduct = jnp.exp(logk[:, c : c + 1])
-        active = (1 - mask[:, c : c + 1]).astype(jnp.float32)
-        heads = [hb[rows * t : rows * (t + 1), c : c + 1] for t in range(tests)]
-        seeds = [active * seed[rows * t : rows * (t + 1), c : c + 1] for t in range(tests)]
-        sides.append((conduct, active, heads, seeds))
+    for c in (0, columns - 1):
+        column = slice(c, c + 1)
+        heads = [hb[rows * t : rows * (t + 1), column] for t in range(tests)]
+        seeds = [active[:, column] * seed[rows * t : rows * (t + 1), column] for t in range(tests)]
+        sides.append((conduct[:, column], active[:, column], heads, seeds))
 
     def packed(side, odd, with_seed):
         conduct, active, heads, seeds = sides[side]
@@ -93,13 +93,21 @@
 
 
 def local_kernel(
-    rows, tests, total_columns, wells, rates, hb, seed, logk, mask, from_left, from_right, own,
-    message, heads_part, adjoint_part, first_out, last_out, side_part, side_first, side_last,
-    right, weighed, cond_c, act_c, gain_c, inv_c, back_c, first_c, last_c,
+    rows, tests, total_columns, wells, rates, hb_all, seed_all, logk_all, mask_all,
+    message, heads_part, adjoint_part, first_out, last_out, to_right, to_left, own,
+    hb, seed, logk, mask, arrived, right, weighed, cond_c, act_c, gain_c, inv_c, back_c, first_c, last_c,
 ):
+    copies = [
+        pltpu.make_async_copy(whole, here, arrived.at[n])
+        for n, (whole, here) in enumerate(((logk_all, logk), (mask_all, mask), (hb_all, hb), (seed_all, seed)))
+    ]
+    for copy in copies:
+        copy.start()
     columns = hb.shape[1]
     tiles = columns // LANES
     field = tests * rows
+    copies[0].wait()
+    copies[1].wait()
     conduct = jnp.exp(logk[...])
     active = (1 - mask[...]).astype(jnp.float32)
     for k in range(tiles):
@@ -122,6 +130,10 @@
     first_end = first[0] + half / cond_rows[0]
     last_end = last[-1] + half / cond_rows[-1]
     across = first[-1]
+
+    copies[2].wait()
+    copies[3].wait()
+    edge_messages(rows, tests, hb, seed, conduct, active, to_right, to_left, own)
 
     lane = lax.broadcasted_iota(jnp.int32, (rows, columns), 1)
     cond_north = pltpu.roll(conduct, columns - 1, 1)
@@ -164,7 +176,8 @@
             given = [source[pl.ds(k * field + i, tests, stride=rows), :] for i in range(rows)]
             values = sweep(gain_k, inv_k, back_k, given)
             for i in range(rows):
-                out[pl.ds(k * field + i, tests, stride=rows), :] = values[i]
+                start = k * field + i * tests
+                out[start : start + tests, :] = values[i]
             dest = 2 * k + core
             message[dest, 0:tests, :] = values[0]
             message[dest, tests : 2 * tests, :] = values[-1]
@@ -173,33 +186,6 @@
             message[dest, 18:19, :] = across[k : k + 1, :]
         first_out[:, lanes] = first_c[pl.ds(k, rows, stride=tiles), :]
         last_out[:, lanes] = last_c[pl.ds(k, rows, stride=tiles), :]
-
-    halo = from_left[...] + from_right[...]
-    mine = own[...]
-    side_lane = lax.broadcasted_iota(jnp.int32, (rows, LANES), 1)
-    outer = side_lane < 2 * tests
-    halo_k = pltpu.roll(halo, LANES - 2 * tests, 1)
-    own_k = pltpu.roll(mine, LANES - 2 * tests, 1)
-    cond_s = jnp.where(outer, pltpu.roll(halo, LANES - 4 * tests, 1), own_k)
-    cond_s = jnp.where(cond_s > 0.0, cond_s, 1.0)
-    act_s = jnp.where(outer, pltpu.roll(halo, LANES - 6 * tests, 1), pltpu.roll(mine, LANES - 4 * tests, 1))
-    side_face = (2.0 * explicit_ratio) * cond_s * halo_k / (cond_s + halo_k)
-    given_s = jnp.where(outer, halo, act_s * side_face * (halo - mine))
-    cond_sr = [cond_s[i : i + 1, :] for i in range(rows)]
-    act_sr = [act_s[i : i + 1, :] for i in range(rows)]
-    gains_s, inv_s, backs_s = eliminate(cond_sr, act_sr)
-    first_s, last_s = responses(gains_s, inv_s, backs_s, act_sr)
-    part_s = sweep(gains_s, inv_s, backs_s, [given_s[i : i + 1, :] for i in range(rows)])
-    for i in range(rows):
-        side_part[i : i + 1, :] = part_s[i]
-        side_first[i : i + 1, :] = first_s[i]
-        side_last[i : i + 1, :] = last_s[i]
-    ends = (
-        part_s[0], part_s[-1], first_s[0] + half / cond_sr[0], last_s[-1] + half / cond_sr[-1], first_s[-1],
-    )
-    for dest in range(2 * tiles):
-        for r, value in enumerate(ends):
-            message[dest, 19 + r : 20 + r, :] = value
 
 
 def chain(first_end, last_end, across, first_value, last_value):
@@ -234,32 +220,60 @@
     return [nothing] + flux[1:] + [nothing]
 
 
-def line_kernel(devices, tests, got, reply, side_flux, held):
-    def solve(first_end, last_end, across, first_value, last_value):
-        def pick(span):
-            return [got[d, span, :] for d in range(devices)]
-
-        return chain(pick(first_end), pick(last_end), pick(across), pick(first_value), pick(last_value))
-
-    side = solve(slice(21, 22), slice(22, 23), slice(23, 24), slice(19, 20), slice(20, 21))
-    for d in range(devices + 1):
-        held[d : d + 1, :] = side[d]
-    flux = solve(slice(16, 17), slice(17, 18), slice(18, 19), slice(0, tests), slice(tests, 2 * tests))
+def side_lanes(rows, tests, from_left, from_right, own, side_part, side_first, side_last):
+    halo = from_left[...] + from_right[...]
+    mine = own[...]
+    side_lane = lax.broadcasted_iota(jnp.int32, (rows, LANES), 1)
+    outer = side_lane < 2 * tests
+    halo_k = pltpu.roll(halo, LANES - 2 * tests, 1)
+    own_k = pltpu.roll(mine, LANES - 2 * tests, 1)
+    cond_s = jnp.where(outer, pltpu.roll(halo, LANES - 4 * tests, 1), own_k)
+    cond_s = jnp.where(cond_s > 0.0, cond_s, 1.0)
+    act_s = jnp.where(outer, pltpu.roll(halo, LANES - 6 * tests, 1), pltpu.roll(mine, LANES - 4 * tests, 1))
+    side_face = (2.0 * explicit_ratio) * cond_s * halo_k / (cond_s + halo_k)
+    given_s = jnp.where(outer, halo, act_s * side_face * (halo - mine))
+    cond_sr = [cond_s[i : i + 1, :] for i in range(rows)]
+    act_sr = [act_s[i : i + 1, :] for i in range(rows)]
+    gains_s, inv_s, backs_s = eliminate(cond_sr, act_sr)
+    first_s, last_s = responses(gains_s, inv_s, backs_s, act_sr)
+    part_s = sweep(gains_s, inv_s, backs_s, [given_s[i : i + 1, :] for i in range(rows)])
+    for i in range(rows):
+        side_part[i : i + 1, :] = part_s[i]
+        side_first[i : i + 1, :] = first_s[i]
+        side_last[i : i + 1, :] = last_s[i]
+    half = 0.5 / implicit_ratio
+    ends = (
+        part_s[0], part_s[-1], first_s[0] + half / cond_sr[0], last_s[-1] + half / cond_sr[-1], first_s[-1],
+    )
+    return ends
+
+
+def line_kernel(devices, rows, tests, got, from_left, from_right, own, reply, side_part, side_first, side_last):
+    def pick(low, high):
+        return [got[d, low:high, :] for d in range(devices)]
+
+    flux = chain(pick(16, 17), pick(17, 18), pick(18, 19), pick(0, tests), pick(tests, 2 * tests))
+    ends = side_lanes(rows, tests, from_left, from_right, own, side_part, side_first, side_last)
     for d in range(devices):
         reply[d, 0:tests, :] = flux[d]
         reply[d, tests : 2 * tests, :] = flux[d + 1]
-    me = lax.axis_index("gx")
-    side_flux[0:1, :] = held[pl.ds(me, 1), :]
-    side_flux[1:2, :] = held[pl.ds(me + 1, 1), :]
+        for r, value in enumerate(ends):
+            reply[d, 16 + r : 17 + r, :] = value
 
 
 def final_kernel(
     rows, tests, hb, logk, heads_part, adjoint_part, first_in, last_in, got, from_left, from_right,
-    side_part, side_first, side_last, side_flux, heads, sensitivity,
+    side_part, side_first, side_last, heads, sensitivity, held,
 ):
     columns = hb.shape[1]
     tiles = columns // LANES
-    side = side_part[...] + side_first[...] * side_flux[0:1, :] - side_last[...] * side_flux[1:2, :]
+    devices = got.shape[0]
+    side_rows = [[got[d, 16 + r : 17 + r, :] for d in range(devices)] for r in range(5)]
+    for d, value in enumerate(chain(side_rows[2], side_rows[3], side_rows[4], side_rows[0], side_rows[1])):
+        held[d : d + 1, :] = value
+    me = lax.axis_index("gx")
+    side_flux = [held[pl.ds(me, 1), :], held[pl.ds(me + 1, 1), :]]
+    side = side_part[...] + side_first[...] * side_flux[0] - side_last[...] * side_flux[1]
     halo = from_left[...] + from_right[...]
     conduct = jnp.exp(logk[...])
     first = first_in[...]
@@ -273,8 +287,8 @@
         return jnp.concatenate([got[2 * k + core, r : r + 1, :] for k in range(tiles)], axis=1)
 
     def joined(part, t):
-        starts = [(k * tests + t) * rows for k in range(tiles)]
-        return jnp.concatenate([part[start : start + rows, :] for start in starts], axis=1)
+        starts = [k * tests * rows + t for k in range(tiles)]
+        return jnp.concatenate([part[pl.ds(start, rows, stride=tests), :] for start in starts], axis=1)
 
     def beside(values, index):
         return values[:, index : index + 1]
@@ -293,7 +307,7 @@
         heads[here, :] = head
         weight = joined(adjoint_part, t) + first * fluxes[1][0] - last * fluxes[1][1]
         for end in (0, 1):
-            side_row = side_flux[end : end + 1, :]
+            side_row = side_flux[end]
             whole = fluxes[0][end] + jnp.where(row_lane == 0, beside(side_row, 2 * tests + t), 0.0)
             whole = whole + jnp.where(row_lane == columns - 1, beside(side_row, 3 * tests + t), 0.0)
             end_products[end] = end_products[end] + whole * fluxes[1][end]
@@ -333,6 +347,7 @@
 
 VMEM = pl.BlockSpec(memory_space=pltpu.VMEM)
 SMEM = pl.BlockSpec(memory_space=pltpu.SMEM)
+LOCAL_LIMIT = 58 * 1024 * 1024
 PARAMS = pltpu.CompilerParams(vmem_limit_bytes=40 * 1024 * 1024)
 
 
@@ -344,54 +359,45 @@
     hb = head_before.reshape(tests * rows, columns)
     seed = adjoint_seed.reshape(tests * rows, columns)
 
-    def ends(height):
-        return [pl.BlockSpec((height, LANES), lambda i, k=k: (0, k)) for k in (0, tiles - 1)]
-
-    small = pl.BlockSpec((rows, LANES), lambda i: (0, 0))
-    to_right, to_left, own = pl.pallas_call(
-        functools.partial(edge_kernel, rows, tests),
-        grid=(1,),
-        in_specs=ends(tests * rows) * 2 + ends(rows) * 2,
-        out_specs=[small] * 3,
-        out_shape=[f32(rows, LANES)] * 3,
-        compiler_params=PARAMS,
-        name="edges",
-    )(hb, hb, seed, seed, log_conductivity, log_conductivity, fixed_mask, fixed_mask)
+    side = f32(rows, LANES)
+    part = f32(tiles * tests * rows, LANES)
+    anywhere = pl.BlockSpec(memory_space=pl.ANY)
+    message, heads_part, adjoint_part, first, last, to_right, to_left, own = pl.pallas_call(
+        functools.partial(local_kernel, rows, tests, columns * peers),
+        in_specs=[SMEM] * 2 + [anywhere] * 4,
+        out_specs=[VMEM] * 8,
+        out_shape=[f32(devices, 24, LANES), part, part] + [f32(rows, columns)] * 2 + [side] * 3,
+        scratch_shapes=[pltpu.VMEM((tests * rows, columns), jnp.float32)] * 2
+        + [pltpu.VMEM((rows, columns), jnp.float32), pltpu.VMEM((rows, columns), jnp.int32)]
+        + [pltpu.SemaphoreType.DMA((4,))]
+        + [pltpu.VMEM((tiles * tests * rows, LANES), jnp.float32)] * 2
+        + [pltpu.VMEM((rows * tiles, LANES), jnp.float32)] * 7,
+        compiler_params=pltpu.CompilerParams(vmem_limit_bytes=LOCAL_LIMIT),
+        name="local",
+    )(well_cells, pump_rates, hb, seed, log_conductivity, fixed_mask)
+    got = lax.all_to_all(message, "gx", 0, 0)
     from_left = lax.ppermute(to_right, "gy", [(i, i + 1) for i in range(peers - 1)])
     from_right = lax.ppermute(to_left, "gy", [(i + 1, i) for i in range(peers - 1)])
-
-    part = f32(tiles * tests * rows, LANES)
-    message, heads_part, adjoint_part, first, last, side_part, side_first, side_last = pl.pallas_call(
-        functools.partial(local_kernel, rows, tests, columns * peers),
-        in_specs=[SMEM] * 2 + [VMEM] * 7,
-        out_specs=[VMEM] * 8,
-        out_shape=[f32(devices, 24, LANES), part, part] + [f32(rows, columns)] * 2 + [f32(rows, LANES)] * 3,
-        scratch_shapes=[pltpu.VMEM((tiles * tests * rows, LANES), jnp.float32)] * 2
-        + [pltpu.VMEM((rows * tiles, LANES), jnp.float32)] * 7,
-        compiler_params=PARAMS,
-        name="local",
-    )(well_cells, pump_rates, hb, seed, log_conductivity, fixed_mask, from_left, from_right, own)
-    got = lax.all_to_all(message, "gx", 0, 0)
-    reply, side_flux = pl.pallas_call(
-        functools.partial(line_kernel, devices, tests),
-        in_specs=[VMEM],
-        out_specs=[VMEM] * 2,
-        out_shape=[f32(devices, 2 * tests, LANES), f32(SUBLANES, LANES)],
-        scratch_shapes=[pltpu.VMEM((devices + SUBLANES, LANES), jnp.float32)],
+    reply, side_part, side_first, side_last = pl.pallas_call(
+        functools.partial(line_kernel, devices, rows, tests),
+        in_specs=[VMEM] * 4,
+        out_specs=[VMEM] * 4,
+        out_shape=[f32(devices, 24, LANES)] + [side] * 3,
         compiler_params=PARAMS,
         name="line",
-    )(got)
+    )(got, from_left, from_right, own)
     answer = lax.all_to_all(reply, "gx", 0, 0)
     heads, sensitivity = pl.pallas_call(
         functools.partial(final_kernel, rows, tests),
-        in_specs=[VMEM] * 13,
+        in_specs=[VMEM] * 12,
         out_specs=[VMEM] * 2,
         out_shape=[f32(tests * rows, columns), f32(rows, columns)],
+        scratch_shapes=[pltpu.VMEM((devices + SUBLANES, LANES), jnp.float32)],
         compiler_params=PARAMS,
         name="final",
     )(
         hb, log_conductivity, heads_part, adjoint_part, first, last, answer, from_left, from_right,
-        side_part, side_first, side_last, side_flux,
+        side_part, side_first, side_last,
     )
     return heads.reshape(tests, rows, columns), sensitivity
 

time: 53.4 us -> 50.6 us (0.948)
  blocking collectives: 30.9 us -> 18.3 us
  starting transfers between devices: 12.9 us -> 20.8 us
  Pallas kernels: 4.03 us -> 6.52 us
  local copies, waits for them, and re-layouts: 3.78 us -> 2.8 us
    all_to_all x1 -> x0, blocking collectives: 18.9 us -> none  [per_device(): got = lax.all_to_all(message, 'gx', 0, 0)]
    all_to_all x0 -> x1, starting transfers between devices: none -> 7.93 us  [per_device(): got = lax.all_to_all(message, 'gx', 0, 0)]
    all_to_all x1, blocking collectives: 12 us -> 18.3 us  [per_device(): answer = lax.all_to_all(reply, 'gx', 0, 0)]
    pallas_call x1, Pallas kernels: 2.2 us -> 4.51 us  [per_device(): pl.pallas_call(functools.partial(local_kernel, rows, tests, columns * pee...]
    unnamed x16 -> x14, local copies, waits for them, and re-layouts: 3.78 us -> 2.8 us
  transfers between devices with their start and end apart: 2 -> 3, of which waited for: 1 -> 1; matrix products, arithmetic and copies ran while one was open for 0% -> 0% of each run, Pallas kernels for 0% -> 0%
where the time goes in v2:
time: 50.6 us; the launch traced here: 50.1 us
  starting transfers between devices  20.8 us (41%)
  blocking collectives  18.3 us (36%)
  Pallas kernels  6.52 us (13%)
  local copies, waits for them, and re-layouts  2.8 us (6%)
  waiting for transfers between devices  0.98 us (2%)
  between operations  0.73 us (1%)
    all_to_all x1, blocking collectives, per_device(): answer = lax.all_to_all(reply, 'gx', 0, 0)  18.3 us
    ppermute x1, starting transfers between devices, per_device(): lax.ppermute(to_left, 'gy', [(i + 1, i) for i in range(peers - 1)])  8.85 us
    all_to_all x1, starting transfers between devices, per_device(): got = lax.all_to_all(message, 'gx', 0, 0)  7.93 us
    pallas_call x1, Pallas kernels, per_device(): pl.pallas_call(functools.partial(local_kernel, rows, tests, columns * pee...  4.51 us
    ppermute x1, starting transfers between devices, per_device(): lax.ppermute(to_right, 'gy', [(i, i + 1) for i in range(peers - 1)])  4.02 us
    unnamed x14, local copies, waits for them, and re-layouts  2.8 us
    pallas_call x1, Pallas kernels, per_device(): pl.pallas_call(functools.partial(final_kernel, rows, tests), in_specs=[VM...  1.7 us
  transfers between devices with their start and end apart: 3, of which 1 were waited for; matrix products, arithmetic and copies ran while one was open for 0% of the time, Pallas kernels for 0%

profile of v2, /device:TPU:7, one launch (start us, length us, event | category | flops | bytes accessed | tf_op | source)
XLA Modules:
  0.0 50.1 jit_solution(1355179128872763777)
XLA Ops:
  0.6 4.5 %local.1 = (f32[16,24,128]{2,1,0:T(8,128)}, f32[1024,128]{1,0:T(8,128)}, f32[1024,128]{1,0:T(8,128)}, f32[16,1024]{1,0:T(8,128)}, f32[16,1024]{1,0:T(8,128)}, /*...) custom-call(s32[8]{0:T(128)} %wells.1, f32[8]{0:T(128)} %rates.1, f32[128,1024]{1,0:T(8,128)} %bitcast.3, ...), custom_call_target="tpu_custom_call" | custom-call | tf_op jit(solution)/shard_map/local/pallas_call | solution.py:365
  5.1 0.0 copy-start
  5.2 7.9 %all-to-all-start = ((f32[16,24,128]{2,1,0:T(8,128)}), f32[16,24,128]{2,1,0:T(8,128)S(1)}, u32[]{:S(2)}, u32[]{:S(2)}) async-start(f32[16,24,128]{2,1,0:T(8,128)} %get-tuple-element.20), calls=%async_computation | async-start | bytes 393216 | tf_op jit(solution)/shard_map/all_to_all | solution.py:378
  13.1 4.0 %collective-permute-start = (f32[16,128]{1,0:T(8,128)}, f32[16,128]{1,0:T(8,128)S(1)}, u32[]{:S(2)}, u32[]{:S(2)}) collective-permute-start(f32[16,128]{1,0:T(8,128)} %get-tuple-element.21), channel_id=1, source_target_pairs={{0,1},{1,2},{2,3},{3,4},{4,5},{5,6},{6,7},{7,8},{8,9},{9,10},{10,1... | collective-permute-start | bytes 24584 | tf_op jit(solution)/shard_map/ppermute | solution.py:379
  17.1 8.9 %collective-permute-start.1 = (f32[16,128]{1,0:T(8,128)}, f32[16,128]{1,0:T(8,128)S(1)}, u32[]{:S(2)}, u32[]{:S(2)}) collective-permute-start(f32[16,128]{1,0:T(8,128)} %get-tuple-element.22), channel_id=1, source_target_pairs={{1,0},{2,1},{3,2},{4,3},{5,4},{6,5},{7,6},{8,7},{9,8},{10,9},{11,1... | collective-permute-start | bytes 24584 | tf_op jit(solution)/shard_map/ppermute | solution.py:380
  26.0 0.0 collective-permute-done.from_left
  26.0 1.0 %collective-permute-done.1.from_right = f32[16,128]{1,0:T(8,128)S(1)} collective-permute-done((f32[16,128]{1,0:T(8,128)}, f32[16,128]{1,0:T(8,128)S(1)}, u32[]{:S(2)}, u32[]{:S(2)}) %collective-permute-start.1) | collective-permute-done | bytes 8224 | tf_op jit(solution)/shard_map/ppermute | solution.py:380
  27.0 0.0 all-to-all-done.got
  27.0 0.0 copy-start.6
  27.0 0.7 %copy-done.6 = f32[16,128]{1,0:T(8,128)S(1)} copy-done((f32[16,128]{1,0:T(8,128)S(1)}, f32[16,128]{1,0:T(8,128)}, u32[]{:S(2)}) %copy-start.6) | copy-done | bytes 8216
  27.7 0.3 line.1
  28.0 0.0 copy-start.3
  28.0 0.0 copy-start.4
  28.0 0.0 copy-start.5
  28.0 18.3 %all_to_all.10.got = f32[16,24,128]{2,1,0:T(8,128)S(1)} all-to-all(f32[16,24,128]{2,1,0:T(8,128)S(1)} %get-tuple-element.24), channel_id=1, replica_groups=mesh['gx'=16,'gy'=32] {'gx'}, dimensions={0} | all-to-all | bytes 393216 | tf_op jit(solution)/shard_map/all_to_all | solution.py:389
  46.3 0.0 copy-done
  46.3 0.0 copy-done.3
  46.3 0.0 copy-done.4
  46.3 0.0 copy-done.5
  46.3 0.0 copy-start.1
  46.3 1.0 %copy-done.1 = f32[1024,128]{1,0:T(8,128)S(1)} copy-done((f32[1024,128]{1,0:T(8,128)S(1)}, f32[1024,128]{1,0:T(8,128)}, u32[]{:S(2)}) %copy-start.1) | copy-done | bytes 524312
  47.4 0.0 copy-start.2
  47.4 1.0 %copy-done.2 = f32[1024,128]{1,0:T(8,128)S(1)} copy-done((f32[1024,128]{1,0:T(8,128)S(1)}, f32[1024,128]{1,0:T(8,128)}, u32[]{:S(2)}) %copy-start.2) | copy-done | bytes 524312
  48.4 1.7 %final.1 = (f32[128,1024]{1,0:T(8,128)}, f32[16,1024]{1,0:T(8,128)}) custom-call(f32[128,1024]{1,0:T(8,128)S(1)} %bitcast.4, f32[16,1024]{1,0:T(8,128)S(1)} %copy-done.3, f32[1024,128]{1,0:T(8,128)S(1)} %copy-done.1, f32[1024,128]{1,0:T(8,128)S(1)} %copy-done.2, f32[16,1024]{1,0:T(8,128)S(1)} %copy-done.4, f32[16,1024]{1,0:T(8,128)S(1)} %copy-done.5, ...), custom_call_target="tpu_custom_call" | custom-call | tf_op jit(solution)/shard_map/final/pallas_call | solution.py:390
Async XLA Ops:
  5.1 41.2 %copy-start = (f32[8,16,1024]{2,1,0:T(8,128)S(1)}, f32[8,16,1024]{2,1,0:T(8,128)}, u32[]{:S(2)}) copy-start(f32[8,16,1024]{2,1,0:T(8,128)} %param.6) | copy-start | bytes 1572868
  5.2 21.8 %all-to-all-start = ((f32[16,24,128]{2,1,0:T(8,128)}), f32[16,24,128]{2,1,0:T(8,128)S(1)}, u32[]{:S(2)}, u32[]{:S(2)}) async-start(f32[16,24,128]{2,1,0:T(8,128)} %get-tuple-element.20), calls=%async_computation | async-start | bytes 393216 | tf_op jit(solution)/shard_map/all_to_all | solution.py:378
  13.1 12.9 %collective-permute-start = (f32[16,128]{1,0:T(8,128)}, f32[16,128]{1,0:T(8,128)S(1)}, u32[]{:S(2)}, u32[]{:S(2)}) collective-permute-start(f32[16,128]{1,0:T(8,128)} %get-tuple-element.21), channel_id=1, source_target_pairs={{0,1},{1,2},{2,3},{3,4},{4,5},{5,6},{6,7},{7,8},{8,9},{9,10},{10,1... | collective-permute-start | bytes 24584 | tf_op jit(solution)/shard_map/ppermute | solution.py:379
  17.1 9.8 %collective-permute-start.1 = (f32[16,128]{1,0:T(8,128)}, f32[16,128]{1,0:T(8,128)S(1)}, u32[]{:S(2)}, u32[]{:S(2)}) collective-permute-start(f32[16,128]{1,0:T(8,128)} %get-tuple-element.22), channel_id=1, source_target_pairs={{1,0},{2,1},{3,2},{4,3},{5,4},{6,5},{7,6},{8,7},{9,8},{10,9},{11,1... | collective-permute-start | bytes 24584 | tf_op jit(solution)/shard_map/ppermute | solution.py:380
  27.0 0.7 %copy-start.6 = (f32[16,128]{1,0:T(8,128)S(1)}, f32[16,128]{1,0:T(8,128)}, u32[]{:S(2)}) copy-start(f32[16,128]{1,0:T(8,128)} %get-tuple-element.23.own) | copy-start | bytes 24580
  28.0 18.3 %copy-start.3 = (f32[16,1024]{1,0:T(8,128)S(1)}, f32[16,1024]{1,0:T(8,128)}, u32[]{:S(2)}) copy-start(f32[16,1024]{1,0:T(8,128)} %logk.1) | copy-start | bytes 196612
  28.0 18.3 %copy-start.4 = (f32[16,1024]{1,0:T(8,128)S(1)}, f32[16,1024]{1,0:T(8,128)}, u32[]{:S(2)}) copy-start(f32[16,1024]{1,0:T(8,128)} %get-tuple-element.18.first_in) | copy-start | bytes 196612
  28.0 18.3 %copy-start.5 = (f32[16,1024]{1,0:T(8,128)S(1)}, f32[16,1024]{1,0:T(8,128)}, u32[]{:S(2)}) copy-start(f32[16,1024]{1,0:T(8,128)} %get-tuple-element.19.last_in) | copy-start | bytes 196612
  46.3 1.0 %copy-start.1 = (f32[1024,128]{1,0:T(8,128)S(1)}, f32[1024,128]{1,0:T(8,128)}, u32[]{:S(2)}) copy-start(f32[1024,128]{1,0:T(8,128)} %get-tuple-element.16.heads_part) | copy-start | bytes 1572868
  47.4 1.0 %copy-start.2 = (f32[1024,128]{1,0:T(8,128)S(1)}, f32[1024,128]{1,0:T(8,128)}, u32[]{:S(2)}) copy-start(f32[1024,128]{1,0:T(8,128)} %get-tuple-element.17.adjoint_part) | copy-start | bytes 1572868

commit v3 on v2

--- a/solution.py
+++ b/solution.py
@@ -93,14 +93,17 @@
 
 
 def local_kernel(
-    rows, tests, total_columns, wells, rates, hb_all, seed_all, logk_all, mask_all,
-    message, heads_part, adjoint_part, first_out, last_out, to_right, to_left, own,
-    hb, seed, logk, mask, arrived, right, weighed, cond_c, act_c, gain_c, inv_c, back_c, first_c, last_c,
+    rows, tests, total_columns, wells_all, rates_all, hb_all, seed_all, logk_all, mask_all,
+    message_all, heads_part, adjoint_part, first_out, last_out, to_right, to_left, own,
+    wells, rates, hb, seed, logk, mask, message, arrived, taken, sent,
+    right, weighed, cond_c, act_c, gain_c, inv_c, back_c, first_c, last_c,
 ):
-    copies = [
-        pltpu.make_async_copy(whole, here, arrived.at[n])
-        for n, (whole, here) in enumerate(((logk_all, logk), (mask_all, mask), (hb_all, hb), (seed_all, seed)))
-    ]
+    pairs = ((logk_all, logk), (mask_all, mask), (wells_all, wells), (rates_all, rates))
+    copies = [pltpu.make_async_copy(whole, here, arrived.at[n]) for n, (whole, here) in enumerate(pairs)]
+    for t in range(tests):
+        here = pl.ds(rows * t, rows)
+        for n, (whole, part) in enumerate(((hb_all, hb), (seed_all, seed))):
+            copies.append(pltpu.make_async_copy(whole.at[here, :], part.at[here, :], taken.at[n, t]))
     for copy in copies:
         copy.start()
     columns = hb.shape[1]
@@ -131,16 +134,14 @@
     last_end = last[-1] + half / cond_rows[-1]
     across = first[-1]
 
-    copies[2].wait()
-    copies[3].wait()
-    edge_messages(rows, tests, hb, seed, conduct, active, to_right, to_left, own)
-
     lane = lax.broadcasted_iota(jnp.int32, (rows, columns), 1)
     cond_north = pltpu.roll(conduct, columns - 1, 1)
     face = (2.0 * explicit_ratio) * conduct * cond_north / (conduct + cond_north)
     face = jnp.where(lane == columns - 1, 0.0, face)
     for t in range(tests):
         here = slice(rows * t, rows * (t + 1))
+        copies[4 + 2 * t].wait()
+        copies[5 + 2 * t].wait()
         head = hb[here, :]
         flow = face * (pltpu.roll(head, columns - 1, 1) - head)
         value = head + active * (flow - pltpu.roll(flow, 1, 1))
@@ -150,6 +151,8 @@
             there = slice(k * field + rows * t, k * field + rows * (t + 1))
             right[there, :] = value[:, lanes]
             weighed[there, :] = seeded[:, lanes]
+    copies[2].wait()
+    copies[3].wait()
     row_start = lax.axis_index("gx") * rows
     column_start = lax.axis_index("gy") * columns
     row_lane = lax.broadcasted_iota(jnp.int32, (1, LANES), 1)
@@ -167,6 +170,7 @@
             added = jnp.where(row_lane == well_column % LANES, act_row * rates[t], 0.0)
             right[there, :] = right[there, :] + added
 
+    sending = []
     for k in range(tiles):
         lanes = slice(k * LANES, (k + 1) * LANES)
         gain_k = [None] + [gain_c[tiles * i + k : tiles * i + k + 1, :] for i in range(1, rows)]
@@ -184,8 +188,14 @@
             message[dest, 16:17, :] = first_end[k : k + 1, :]
             message[dest, 17:18, :] = last_end[k : k + 1, :]
             message[dest, 18:19, :] = across[k : k + 1, :]
+        both = pl.ds(2 * k, 2)
+        sending.append(pltpu.make_async_copy(message.at[both], message_all.at[both], sent.at[k]))
+        sending[-1].start()
         first_out[:, lanes] = first_c[pl.ds(k, rows, stride=tiles), :]
         last_out[:, lanes] = last_c[pl.ds(k, rows, stride=tiles), :]
+    edge_messages(rows, tests, hb, seed, conduct, active, to_right, to_left, own)
+    for copy in sending:
+        copy.wait()
 
 
 def chain(first_end, last_end, across, first_value, last_value):
@@ -263,7 +273,7 @@
 
 def final_kernel(
     rows, tests, hb, logk, heads_part, adjoint_part, first_in, last_in, got, from_left, from_right,
-    side_part, side_first, side_last, heads, sensitivity, held,
+    side_part, side_first, side_last, heads_all, sensitivity, heads, sent, held,
 ):
     columns = hb.shape[1]
     tiles = columns // LANES
@@ -298,13 +308,17 @@
     along_rows = jnp.zeros((rows, columns), jnp.float32)
     along_columns = jnp.zeros((rows, columns), jnp.float32)
     start_face = jnp.zeros((rows, LANES), jnp.float32)
+    sending = []
     for t in range(tests):
         here = slice(rows * t, rows * (t + 1))
+        block = pl.ds(rows * t, rows)
         fluxes = [[wide(core, base + t) for base in (0, tests)] for core in (0, 1)]
         head = joined(heads_part, t) + first * fluxes[0][0] - last * fluxes[0][1]
         head = head + jnp.where(at_start, beside(side, 2 * tests + t), 0.0)
         head = head + jnp.where(at_end, beside(side, 3 * tests + t), 0.0)
         heads[here, :] = head
+        sending.append(pltpu.make_async_copy(heads.at[block, :], heads_all.at[block, :], sent.at[t]))
+        sending[-1].start()
         weight = joined(adjoint_part, t) + first * fluxes[1][0] - last * fluxes[1][1]
         for end in (0, 1):
             side_row = side_flux[end]
@@ -339,6 +353,12 @@
     total = total + jnp.where(row == 0, scale * end_products[0], 0.0)
     total = total + jnp.where(row == rows - 1, scale * end_products[1], 0.0)
     sensitivity[...] = total * (0.5 / conduct)
+    for copy in sending:
+        copy.wait()
+
+
+def in_hbm(x):
+    return pltpu.with_memory_space_constraint(x, pltpu.HBM)
 
 
 def f32(*shape):
@@ -346,8 +366,6 @@
 
 
 VMEM = pl.BlockSpec(memory_space=pltpu.VMEM)
-SMEM = pl.BlockSpec(memory_space=pltpu.SMEM)
-LOCAL_LIMIT = 58 * 1024 * 1024
 PARAMS = pltpu.CompilerParams(vmem_limit_bytes=40 * 1024 * 1024)
 
 
@@ -364,17 +382,19 @@
     anywhere = pl.BlockSpec(memory_space=pl.ANY)
     message, heads_part, adjoint_part, first, last, to_right, to_left, own = pl.pallas_call(
         functools.partial(local_kernel, rows, tests, columns * peers),
-        in_specs=[SMEM] * 2 + [anywhere] * 4,
-        out_specs=[VMEM] * 8,
+        in_specs=[anywhere] * 6,
+        out_specs=[anywhere] + [VMEM] * 7,
         out_shape=[f32(devices, 24, LANES), part, part] + [f32(rows, columns)] * 2 + [side] * 3,
-        scratch_shapes=[pltpu.VMEM((tests * rows, columns), jnp.float32)] * 2
+        scratch_shapes=[pltpu.SMEM((tests,), jnp.int32), pltpu.SMEM((tests,), jnp.float32)]
+        + [pltpu.VMEM((tests * rows, columns), jnp.float32)] * 2
         + [pltpu.VMEM((rows, columns), jnp.float32), pltpu.VMEM((rows, columns), jnp.int32)]
-        + [pltpu.SemaphoreType.DMA((4,))]
+        + [pltpu.VMEM((devices, 24, LANES), jnp.float32)]
+        + [pltpu.SemaphoreType.DMA((4,)), pltpu.SemaphoreType.DMA((2, tests)), pltpu.SemaphoreType.DMA((tiles,))]
         + [pltpu.VMEM((tiles * tests * rows, LANES), jnp.float32)] * 2
         + [pltpu.VMEM((rows * tiles, LANES), jnp.float32)] * 7,
-        compiler_params=pltpu.CompilerParams(vmem_limit_bytes=LOCAL_LIMIT),
+        compiler_params=PARAMS,
         name="local",
-    )(well_cells, pump_rates, hb, seed, log_conductivity, fixed_mask)
+    )(*[in_hbm(x) for x in (well_cells, pump_rates, hb, seed, log_conductivity, fixed_mask)])
     got = lax.all_to_all(message, "gx", 0, 0)
     from_left = lax.ppermute(to_right, "gy", [(i, i + 1) for i in range(peers - 1)])
     from_right = lax.ppermute(to_left, "gy", [(i + 1, i) for i in range(peers - 1)])
@@ -390,9 +410,10 @@
     heads, sensitivity = pl.pallas_call(
         functools.partial(final_kernel, rows, tests),
         in_specs=[VMEM] * 12,
-        out_specs=[VMEM] * 2,
+        out_specs=[anywhere, VMEM],
         out_shape=[f32(tests * rows, columns), f32(rows, columns)],
-        scratch_shapes=[pltpu.VMEM((devices + SUBLANES, LANES), jnp.float32)],
+        scratch_shapes=[pltpu.VMEM((tests * rows, columns), jnp.float32), pltpu.SemaphoreType.DMA((tests,))]
+        + [pltpu.VMEM((devices + SUBLANES, LANES), jnp.float32)],
         compiler_params=PARAMS,
         name="final",
     )(

time: 50.6 us -> 47.7 us (0.943)
  local copies, waits for them, and re-layouts: 2.8 us -> 0.01 us
    unnamed x14 -> x4, local copies, waits for them, and re-layouts: 2.8 us -> 0.01 us
where the time goes in v3:
time: 47.7 us; the launch traced here: 47.3 us
  starting transfers between devices  20.8 us (44%)
  blocking collectives  18.3 us (38%)
  Pallas kernels  6.78 us (14%)
  waiting for transfers between devices  0.77 us (2%)
  between operations  0.69 us (1%)
    all_to_all x1, blocking collectives, per_device(): answer = lax.all_to_all(reply, 'gx', 0, 0)  18.3 us
    ppermute x1, starting transfers between devices, per_device(): lax.ppermute(to_left, 'gy', [(i + 1, i) for i in range(peers - 1)])  8.85 us
    all_to_all x1, starting transfers between devices, per_device(): got = lax.all_to_all(message, 'gx', 0, 0)  7.93 us
    pallas_call x1, Pallas kernels, per_device(): pl.pallas_call(functools.partial(local_kernel, rows, tests, columns * pee...  4.31 us
    ppermute x1, starting transfers between devices, per_device(): lax.ppermute(to_right, 'gy', [(i, i + 1) for i in range(peers - 1)])  4.02 us
    pallas_call x1, Pallas kernels, per_device(): pl.pallas_call(functools.partial(final_kernel, rows, tests), in_specs=[VM...  2.16 us
  transfers between devices with their start and end apart: 3, of which 1 were waited for; matrix products, arithmetic and copies ran while one was open for 0% of the time, Pallas kernels for 0%

profile of v3, /device:TPU:7, one launch (start us, length us, event | category | flops | bytes accessed | tf_op | source)
XLA Modules:
  0.0 47.3 jit_solution(4637575250043424770)
XLA Ops:
  0.6 4.3 %local.1 = (f32[16,24,128]{2,1,0:T(8,128)}, f32[1024,128]{1,0:T(8,128)S(1)}, f32[1024,128]{1,0:T(8,128)S(1)}, f32[16,1024]{1,0:T(8,128)S(1)}, f32[16,1024]{1,0:T...) custom-call(s32[8]{0:T(128)} %wells_all.1, f32[8]{0:T(128)} %rates_all.1, ...), custom_call_target="tpu_custom_call" | custom-call | tf_op jit(solution)/shard_map/local/pallas_call | solution.py:383
  4.9 0.0 copy-start
  5.0 7.9 %all-to-all-start = ((f32[16,24,128]{2,1,0:T(8,128)}), f32[16,24,128]{2,1,0:T(8,128)S(1)}, u32[]{:S(2)}, u32[]{:S(2)}) async-start(f32[16,24,128]{2,1,0:T(8,128)} %get-tuple-element.20), calls=%async_computation | async-start | bytes 393216 | tf_op jit(solution)/shard_map/all_to_all | solution.py:398
  12.9 4.0 %collective-permute-start = (f32[16,128]{1,0:T(8,128)S(1)}, f32[16,128]{1,0:T(8,128)S(1)}, u32[]{:S(2)}, u32[]{:S(2)}) collective-permute-start(f32[16,128]{1,0:T(8,128)S(1)} %get-tuple-element.21), channel_id=1, source_target_pairs={{0,1},{1,2},{2,3},{3,4},{4,5},{5,6},{6,7},{7,8},{8,9},{9,10},{10,1... | collective-permute-start | bytes 24584 | tf_op jit(solution)/shard_map/ppermute | solution.py:399
  16.9 8.9 %collective-permute-start.1 = (f32[16,128]{1,0:T(8,128)S(1)}, f32[16,128]{1,0:T(8,128)S(1)}, u32[]{:S(2)}, u32[]{:S(2)}) collective-permute-start(f32[16,128]{1,0:T(8,128)S(1)} %get-tuple-element.22), channel_id=1, source_target_pairs={{1,0},{2,1},{3,2},{4,3},{5,4},{6,5},{7,6},{8,7},{9,8},{10,9},{11,1... | collective-permute-start | bytes 24584 | tf_op jit(solution)/shard_map/ppermute | solution.py:400
  25.8 0.0 collective-permute-done.from_left
  25.8 0.8 %collective-permute-done.1.from_right = f32[16,128]{1,0:T(8,128)S(1)} collective-permute-done((f32[16,128]{1,0:T(8,128)S(1)}, f32[16,128]{1,0:T(8,128)S(1)}, u32[]{:S(2)}, u32[]{:S(2)}) %collective-permute-start.1) | collective-permute-done | bytes 8224 | tf_op jit(solution)/shard_map/ppermute | solution.py:400
  26.6 0.0 all-to-all-done.got
  26.6 0.3 line.1
  26.9 0.0 copy-start.1
  26.9 18.3 %all_to_all.10.got = f32[16,24,128]{2,1,0:T(8,128)S(1)} all-to-all(f32[16,24,128]{2,1,0:T(8,128)S(1)} %get-tuple-element.24), channel_id=1, replica_groups=mesh['gx'=16,'gy'=32] {'gx'}, dimensions={0} | all-to-all | bytes 393216 | tf_op jit(solution)/shard_map/all_to_all | solution.py:409
  45.2 0.0 copy-done
  45.2 0.0 copy-done.1
  45.2 2.2 %final.1 = (f32[128,1024]{1,0:T(8,128)}, f32[16,1024]{1,0:T(8,128)}) custom-call(f32[128,1024]{1,0:T(8,128)S(1)} %bitcast.4, f32[16,1024]{1,0:T(8,128)S(1)} %copy-done.1, f32[1024,128]{1,0:T(8,128)S(1)} %get-tuple-element.16.heads_part, f32[1024,128]{1,0:T(8,128)S(1)} %get-tuple-element.17.adjoint_part, f32[16,1024]{1,0:T(8,128)S(1)} %get-tuple-element.18.first_in, ...), custom_call_target="tpu_custom_call" | custom-call | tf_op jit(solution)/shard_map/final/pallas_call | solution.py:410
Async XLA Ops:
  4.9 40.2 %copy-start = (f32[8,16,1024]{2,1,0:T(8,128)S(1)}, f32[8,16,1024]{2,1,0:T(8,128)}, u32[]{:S(2)}) copy-start(f32[8,16,1024]{2,1,0:T(8,128)} %param.6) | copy-start | bytes 1572868
  5.0 21.6 %all-to-all-start = ((f32[16,24,128]{2,1,0:T(8,128)}), f32[16,24,128]{2,1,0:T(8,128)S(1)}, u32[]{:S(2)}, u32[]{:S(2)}) async-start(f32[16,24,128]{2,1,0:T(8,128)} %get-tuple-element.20), calls=%async_computation | async-start | bytes 393216 | tf_op jit(solution)/shard_map/all_to_all | solution.py:398
  12.9 12.9 %collective-permute-start = (f32[16,128]{1,0:T(8,128)S(1)}, f32[16,128]{1,0:T(8,128)S(1)}, u32[]{:S(2)}, u32[]{:S(2)}) collective-permute-start(f32[16,128]{1,0:T(8,128)S(1)} %get-tuple-element.21), channel_id=1, source_target_pairs={{0,1},{1,2},{2,3},{3,4},{4,5},{5,6},{6,7},{7,8},{8,9},{9,10},{10,1... | collective-permute-start | bytes 24584 | tf_op jit(solution)/shard_map/ppermute | solution.py:399
  16.9 9.6 %collective-permute-start.1 = (f32[16,128]{1,0:T(8,128)S(1)}, f32[16,128]{1,0:T(8,128)S(1)}, u32[]{:S(2)}, u32[]{:S(2)}) collective-permute-start(f32[16,128]{1,0:T(8,128)S(1)} %get-tuple-element.22), channel_id=1, source_target_pairs={{1,0},{2,1},{3,2},{4,3},{5,4},{6,5},{7,6},{8,7},{9,8},{10,9},{11,1... | collective-permute-start | bytes 24584 | tf_op jit(solution)/shard_map/ppermute | solution.py:400
  26.9 18.3 %copy-start.1 = (f32[16,1024]{1,0:T(8,128)S(1)}, f32[16,1024]{1,0:T(8,128)}, u32[]{:S(2)}) copy-start(f32[16,1024]{1,0:T(8,128)} %logk.1) | copy-start | bytes 196612

commit v4 on v2

--- a/solution.py
+++ b/solution.py
@@ -93,14 +93,15 @@
 
 
 def local_kernel(
-    rows, tests, total_columns, wells, rates, hb_all, seed_all, logk_all, mask_all,
-    message, heads_part, adjoint_part, first_out, last_out, to_right, to_left, own,
-    hb, seed, logk, mask, arrived, right, weighed, cond_c, act_c, gain_c, inv_c, back_c, first_c, last_c,
+    rows, tests, total_columns, wells_all, rates_all, hb_all, seed_all, logk_all, mask_all,
+    message_all, heads_part, adjoint_part, first_out, last_out, to_right, to_left, own,
+    wells, rates, hb, seed, logk, mask, message, arrived, sent,
+    right, weighed, cond_c, act_c, gain_c, inv_c, back_c, first_c, last_c,
 ):
-    copies = [
-        pltpu.make_async_copy(whole, here, arrived.at[n])
-        for n, (whole, here) in enumerate(((logk_all, logk), (mask_all, mask), (hb_all, hb), (seed_all, seed)))
-    ]
+    pairs = (
+        (logk_all, logk), (mask_all, mask), (hb_all, hb), (seed_all, seed), (wells_all, wells), (rates_all, rates),
+    )
+    copies = [pltpu.make_async_copy(whole, here, arrived.at[n]) for n, (whole, here) in enumerate(pairs)]
     for copy in copies:
         copy.start()
     columns = hb.shape[1]
@@ -133,8 +134,6 @@
 
     copies[2].wait()
     copies[3].wait()
-    edge_messages(rows, tests, hb, seed, conduct, active, to_right, to_left, own)
-
     lane = lax.broadcasted_iota(jnp.int32, (rows, columns), 1)
     cond_north = pltpu.roll(conduct, columns - 1, 1)
     face = (2.0 * explicit_ratio) * conduct * cond_north / (conduct + cond_north)
@@ -150,6 +149,8 @@
             there = slice(k * field + rows * t, k * field + rows * (t + 1))
             right[there, :] = value[:, lanes]
             weighed[there, :] = seeded[:, lanes]
+    copies[4].wait()
+    copies[5].wait()
     row_start = lax.axis_index("gx") * rows
     column_start = lax.axis_index("gy") * columns
     row_lane = lax.broadcasted_iota(jnp.int32, (1, LANES), 1)
@@ -178,14 +179,17 @@
             for i in range(rows):
                 start = k * field + i * tests
                 out[start : start + tests, :] = values[i]
-            dest = 2 * k + core
-            message[dest, 0:tests, :] = values[0]
-            message[dest, tests : 2 * tests, :] = values[-1]
-            message[dest, 16:17, :] = first_end[k : k + 1, :]
-            message[dest, 17:18, :] = last_end[k : k + 1, :]
-            message[dest, 18:19, :] = across[k : k + 1, :]
+            start = (2 * k + core) * (2 * tests + 3)
+            message[start : start + tests, :] = values[0]
+            message[start + tests : start + 2 * tests, :] = values[-1]
+            for r, value in enumerate((first_end, last_end, across)):
+                message[start + 2 * tests + r : start + 2 * tests + r + 1, :] = value[k : k + 1, :]
         first_out[:, lanes] = first_c[pl.ds(k, rows, stride=tiles), :]
         last_out[:, lanes] = last_c[pl.ds(k, rows, stride=tiles), :]
+    sending = pltpu.make_async_copy(message, message_all, sent)
+    sending.start()
+    edge_messages(rows, tests, hb, seed, conduct, active, to_right, to_left, own)
+    sending.wait()
 
 
 def chain(first_end, last_end, across, first_value, last_value):
@@ -249,16 +253,25 @@
 
 
 def line_kernel(devices, rows, tests, got, from_left, from_right, own, reply, side_part, side_first, side_last):
+    out_rows, back_rows = 2 * tests + 3, 2 * tests + 2
+
     def pick(low, high):
-        return [got[d, low:high, :] for d in range(devices)]
-
-    flux = chain(pick(16, 17), pick(17, 18), pick(18, 19), pick(0, tests), pick(tests, 2 * tests))
-    ends = side_lanes(rows, tests, from_left, from_right, own, side_part, side_first, side_last)
+        return [got[out_rows * d + low : out_rows * d + high, :] for d in range(devices)]
+
+    ends = [pick(2 * tests + r, 2 * tests + r + 1) for r in range(3)]
+    flux = chain(*ends, pick(0, tests), pick(tests, 2 * tests))
+    side = side_lanes(rows, tests, from_left, from_right, own, side_part, side_first, side_last)
+    width = 4 * tests
+    lane = lax.broadcasted_iota(jnp.int32, (1, LANES), 1)
+    joined = side[0]
+    for r in range(1, 4):
+        joined = jnp.where(lane >= width * r, pltpu.roll(side[r], width * r, 1), joined)
     for d in range(devices):
-        reply[d, 0:tests, :] = flux[d]
-        reply[d, tests : 2 * tests, :] = flux[d + 1]
-        for r, value in enumerate(ends):
-            reply[d, 16 + r : 17 + r, :] = value
+        start = back_rows * d
+        reply[start : start + tests, :] = flux[d]
+        reply[start + tests : start + 2 * tests, :] = flux[d + 1]
+        reply[start + 2 * tests : start + 2 * tests + 1, :] = joined
+        reply[start + 2 * tests + 1 : start + back_rows, :] = side[4]
 
 
 def final_kernel(
@@ -267,9 +280,17 @@
 ):
     columns = hb.shape[1]
     tiles = columns // LANES
-    devices = got.shape[0]
-    side_rows = [[got[d, 16 + r : 17 + r, :] for d in range(devices)] for r in range(5)]
-    for d, value in enumerate(chain(side_rows[2], side_rows[3], side_rows[4], side_rows[0], side_rows[1])):
+    back_rows = 2 * tests + 2
+    devices = got.shape[0] // back_rows
+    width = 4 * tests
+
+    def sent_row(r):
+        return jnp.concatenate([got[back_rows * d + r : back_rows * d + r + 1, :] for d in range(devices)], axis=0)
+
+    packed = sent_row(2 * tests)
+    ends = [packed] + [pltpu.roll(packed, LANES - width * r, 1) for r in range(1, 4)] + [sent_row(2 * tests + 1)]
+    ends = [[value[d : d + 1, :] for d in range(devices)] for value in ends]
+    for d, value in enumerate(chain(ends[2], ends[3], ends[4], ends[0], ends[1])):
         held[d : d + 1, :] = value
     me = lax.axis_index("gx")
     side_flux = [held[pl.ds(me, 1), :], held[pl.ds(me + 1, 1), :]]
@@ -284,7 +305,8 @@
     at_end = lane == columns - 1
 
     def wide(core, r):
-        return jnp.concatenate([got[2 * k + core, r : r + 1, :] for k in range(tiles)], axis=1)
+        starts = [back_rows * (2 * k + core) for k in range(tiles)]
+        return jnp.concatenate([got[starts[k] + r : starts[k] + r + 1, :] for k in range(tiles)], axis=1)
 
     def joined(part, t):
         starts = [k * tests * rows + t for k in range(tiles)]
@@ -341,13 +363,15 @@
     sensitivity[...] = total * (0.5 / conduct)
 
 
+def in_hbm(x):
+    return pltpu.with_memory_space_constraint(x, pltpu.HBM)
+
+
 def f32(*shape):
     return jax.ShapeDtypeStruct(shape, jnp.float32)
 
 
 VMEM = pl.BlockSpec(memory_space=pltpu.VMEM)
-SMEM = pl.BlockSpec(memory_space=pltpu.SMEM)
-LOCAL_LIMIT = 58 * 1024 * 1024
 PARAMS = pltpu.CompilerParams(vmem_limit_bytes=40 * 1024 * 1024)
 
 
@@ -361,32 +385,41 @@
 
     side = f32(rows, LANES)
     part = f32(tiles * tests * rows, LANES)
+    out_rows = 2 * tests + 3
+    back_rows = 2 * tests + 2
+
+    def exchanged(rows_of_all):
+        flat = rows_of_all.reshape(devices, 1, rows_of_all.size // devices)
+        return lax.all_to_all(flat, "gx", 0, 0).reshape(rows_of_all.shape)
+
     anywhere = pl.BlockSpec(memory_space=pl.ANY)
     message, heads_part, adjoint_part, first, last, to_right, to_left, own = pl.pallas_call(
         functools.partial(local_kernel, rows, tests, columns * peers),
-        in_specs=[SMEM] * 2 + [anywhere] * 4,
-        out_specs=[VMEM] * 8,
-        out_shape=[f32(devices, 24, LANES), part, part] + [f32(rows, columns)] * 2 + [side] * 3,
-        scratch_shapes=[pltpu.VMEM((tests * rows, columns), jnp.float32)] * 2
+        in_specs=[anywhere] * 6,
+        out_specs=[anywhere] + [VMEM] * 7,
+        out_shape=[f32(devices * out_rows, LANES), part, part] + [f32(rows, columns)] * 2 + [side] * 3,
+        scratch_shapes=[pltpu.SMEM((tests,), jnp.int32), pltpu.SMEM((tests,), jnp.float32)]
+        + [pltpu.VMEM((tests * rows, columns), jnp.float32)] * 2
         + [pltpu.VMEM((rows, columns), jnp.float32), pltpu.VMEM((rows, columns), jnp.int32)]
-        + [pltpu.SemaphoreType.DMA((4,))]
+        + [pltpu.VMEM((devices * out_rows, LANES), jnp.float32)]
+        + [pltpu.SemaphoreType.DMA((6,)), pltpu.SemaphoreType.DMA]
         + [pltpu.VMEM((tiles * tests * rows, LANES), jnp.float32)] * 2
         + [pltpu.VMEM((rows * tiles, LANES), jnp.float32)] * 7,
-        compiler_params=pltpu.CompilerParams(vmem_limit_bytes=LOCAL_LIMIT),
+        compiler_params=PARAMS,
         name="local",
-    )(well_cells, pump_rates, hb, seed, log_conductivity, fixed_mask)
-    got = lax.all_to_all(message, "gx", 0, 0)
+    )(*[in_hbm(x) for x in (well_cells, pump_rates, hb, seed, log_conductivity, fixed_mask)])
+    got = exchanged(message)
+    from_right = lax.ppermute(to_left, "gy", [(i + 1, i) for i in range(peers - 1)])
     from_left = lax.ppermute(to_right, "gy", [(i, i + 1) for i in range(peers - 1)])
-    from_right = lax.ppermute(to_left, "gy", [(i + 1, i) for i in range(peers - 1)])
     reply, side_part, side_first, side_last = pl.pallas_call(
         functools.partial(line_kernel, devices, rows, tests),
         in_specs=[VMEM] * 4,
         out_specs=[VMEM] * 4,
-        out_shape=[f32(devices, 24, LANES)] + [side] * 3,
+        out_shape=[f32(devices * back_rows, LANES)] + [side] * 3,
         compiler_params=PARAMS,
         name="line",
     )(got, from_left, from_right, own)
-    answer = lax.all_to_all(reply, "gx", 0, 0)
+    answer = exchanged(reply)
     heads, sensitivity = pl.pallas_call(
         functools.partial(final_kernel, rows, tests),
         in_specs=[VMEM] * 12,

time: 50.6 us -> 45.2 us (0.89)
  local copies, waits for them, and re-layouts: 2.8 us -> 0.01 us
  Pallas kernels: 6.52 us -> 5.34 us
  blocking collectives: 18.3 us -> 17.3 us
    unnamed x14 -> x4, local copies, waits for them, and re-layouts: 2.8 us -> 0.01 us
    pallas_call x1, Pallas kernels: 4.51 us -> 3.35 us  [per_device(): pl.pallas_call(functools.partial(local_kernel, rows, tests, columns * pee...]
    all_to_all x1, blocking collectives: 18.3 us -> 17.3 us  [exchanged(): return lax.all_to_all(flat, 'gx', 0, 0).reshape(rows_of_all.shape)]
where the time goes in v4:
time: 45.2 us; the launch traced here: 44.9 us
  starting transfers between devices  20.8 us (46%)
  blocking collectives  17.3 us (38%)
  Pallas kernels  5.34 us (12%)
  waiting for transfers between devices  0.77 us (2%)
  between operations  0.67 us (1%)
    all_to_all x1, blocking collectives, exchanged(): return lax.all_to_all(flat, 'gx', 0, 0).reshape(rows_of_all.shape)  17.3 us
    ppermute x1, starting transfers between devices, per_device(): lax.ppermute(to_left, 'gy', [(i + 1, i) for i in range(peers - 1)])  8.85 us
    all_to_all x1, starting transfers between devices, exchanged(): return lax.all_to_all(flat, 'gx', 0, 0).reshape(rows_of_all.shape)  7.93 us
    ppermute x1, starting transfers between devices, per_device(): lax.ppermute(to_right, 'gy', [(i, i + 1) for i in range(peers - 1)])  4.02 us
    pallas_call x1, Pallas kernels, per_device(): pl.pallas_call(functools.partial(local_kernel, rows, tests, columns * pee...  3.35 us
    pallas_call x1, Pallas kernels, per_device(): pl.pallas_call(functools.partial(final_kernel, rows, tests), in_specs=[VM...  1.63 us
  transfers between devices with their start and end apart: 3, of which 1 were waited for; matrix products, arithmetic and copies ran while one was open for 0% of the time, Pallas kernels for 0%

profile of v4, /device:TPU:7, one launch (start us, length us, event | category | flops | bytes accessed | tf_op | source)
XLA Modules:
  0.0 44.9 jit_solution(1851420071092917608)
XLA Ops:
  0.6 3.3 %local.1 = (f32[304,128]{1,0:T(8,128)}, f32[1024,128]{1,0:T(8,128)S(1)}, f32[1024,128]{1,0:T(8,128)S(1)}, f32[16,1024]{1,0:T(8,128)S(1)}, f32[16,1024]{1,0:T(8,1...) custom-call(s32[8]{0:T(128)} %wells_all.1, f32[8]{0:T(128)} %rates_all.1, ...), custom_call_target="tpu_custom_call" | custom-call | tf_op jit(solution)/shard_map/local/pallas_call | solution.py:396
  4.0 0.0 copy-start
  4.0 7.9 %all-to-all-start = ((f32[16,1,2432]{2,1,0:T(1,128)}), f32[16,1,2432]{2,1,0:T(1,128)S(1)}, u32[]{:S(2)}, u32[]{:S(2)}) async-start(f32[16,1,2432]{2,1,0:T(1,128)} %bitcast.2), calls=%async_computation | async-start | bytes 311296 | tf_op jit(solution)/shard_map/all_to_all | solution.py:393
  11.9 4.0 %collective-permute-start = (f32[16,128]{1,0:T(8,128)S(1)}, f32[16,128]{1,0:T(8,128)S(1)}, u32[]{:S(2)}, u32[]{:S(2)}) collective-permute-start(f32[16,128]{1,0:T(8,128)S(1)} %get-tuple-element.21), channel_id=1, source_target_pairs={{0,1},{1,2},{2,3},{3,4},{4,5},{5,6},{6,7},{7,8},{8,9},{9,10},{10,1... | collective-permute-start | bytes 24584 | tf_op jit(solution)/shard_map/ppermute | solution.py:413
  16.0 8.9 %collective-permute-start.1 = (f32[16,128]{1,0:T(8,128)S(1)}, f32[16,128]{1,0:T(8,128)S(1)}, u32[]{:S(2)}, u32[]{:S(2)}) collective-permute-start(f32[16,128]{1,0:T(8,128)S(1)} %get-tuple-element.22), channel_id=1, source_target_pairs={{1,0},{2,1},{3,2},{4,3},{5,4},{6,5},{7,6},{8,7},{9,8},{10,9},{11,1... | collective-permute-start | bytes 24584 | tf_op jit(solution)/shard_map/ppermute | solution.py:412
  24.8 0.0 collective-permute-done.from_left
  24.8 0.8 %collective-permute-done.1.from_right = f32[16,128]{1,0:T(8,128)S(1)} collective-permute-done((f32[16,128]{1,0:T(8,128)S(1)}, f32[16,128]{1,0:T(8,128)S(1)}, u32[]{:S(2)}, u32[]{:S(2)}) %collective-permute-start.1) | collective-permute-done | bytes 8224 | tf_op jit(solution)/shard_map/ppermute | solution.py:412
  25.6 0.0 all-to-all-done
  25.6 0.4 line.1
  26.0 0.0 copy-start.1
  26.0 17.3 %all_to_all.10 = f32[16,1,2304]{2,1,0:T(1,128)S(1)} all-to-all(f32[16,1,2304]{2,1,0:T(1,128)S(1)} %bitcast.11), channel_id=1, replica_groups=mesh['gx'=16,'gy'=32] {'gx'}, dimensions={0} | all-to-all | bytes 294912 | tf_op jit(solution)/shard_map/all_to_all | solution.py:393
  43.3 0.0 copy-done
  43.3 0.0 copy-done.1
  43.3 1.6 %final.1 = (f32[128,1024]{1,0:T(8,128)}, f32[16,1024]{1,0:T(8,128)}) custom-call(f32[128,1024]{1,0:T(8,128)S(1)} %bitcast.8, f32[16,1024]{1,0:T(8,128)S(1)} %copy-done.1, f32[1024,128]{1,0:T(8,128)S(1)} %get-tuple-element.16.heads_part, f32[1024,128]{1,0:T(8,128)S(1)} %get-tuple-element.17.adjoint_part, f32[16,1024]{1,0:T(8,128)S(1)} %get-tuple-element.18.first_in, ...), custom_call_target="tpu_custom_call" | custom-call | tf_op jit(solution)/shard_map/final/pallas_call | solution.py:423
Async XLA Ops:
  4.0 39.3 %copy-start = (f32[8,16,1024]{2,1,0:T(8,128)S(1)}, f32[8,16,1024]{2,1,0:T(8,128)}, u32[]{:S(2)}) copy-start(f32[8,16,1024]{2,1,0:T(8,128)} %param.6) | copy-start | bytes 1572868
  4.0 21.6 %all-to-all-start = ((f32[16,1,2432]{2,1,0:T(1,128)}), f32[16,1,2432]{2,1,0:T(1,128)S(1)}, u32[]{:S(2)}, u32[]{:S(2)}) async-start(f32[16,1,2432]{2,1,0:T(1,128)} %bitcast.2), calls=%async_computation | async-start | bytes 311296 | tf_op jit(solution)/shard_map/all_to_all | solution.py:393
  11.9 12.9 %collective-permute-start = (f32[16,128]{1,0:T(8,128)S(1)}, f32[16,128]{1,0:T(8,128)S(1)}, u32[]{:S(2)}, u32[]{:S(2)}) collective-permute-start(f32[16,128]{1,0:T(8,128)S(1)} %get-tuple-element.21), channel_id=1, source_target_pairs={{0,1},{1,2},{2,3},{3,4},{4,5},{5,6},{6,7},{7,8},{8,9},{9,10},{10,1... | collective-permute-start | bytes 24584 | tf_op jit(solution)/shard_map/ppermute | solution.py:413
  16.0 9.6 %collective-permute-start.1 = (f32[16,128]{1,0:T(8,128)S(1)}, f32[16,128]{1,0:T(8,128)S(1)}, u32[]{:S(2)}, u32[]{:S(2)}) collective-permute-start(f32[16,128]{1,0:T(8,128)S(1)} %get-tuple-element.22), channel_id=1, source_target_pairs={{1,0},{2,1},{3,2},{4,3},{5,4},{6,5},{7,6},{8,7},{9,8},{10,9},{11,1... | collective-permute-start | bytes 24584 | tf_op jit(solution)/shard_map/ppermute | solution.py:412
  26.0 17.3 %copy-start.1 = (f32[16,1024]{1,0:T(8,128)S(1)}, f32[16,1024]{1,0:T(8,128)}, u32[]{:S(2)}) copy-start(f32[16,1024]{1,0:T(8,128)} %logk.1) | copy-start | bytes 196612

commit v5 on v4

--- a/solution.py
+++ b/solution.py
@@ -46,23 +46,23 @@
 
 def eliminate(conduct, active):
     rows = len(conduct)
-    gains, inverses, backs = [None], [], []
-    excess = jnp.ones_like(conduct[0])
-    face = None
+    faces = [
+        (2.0 * implicit_ratio) * conduct[i] * conduct[i + 1] / (conduct[i] + conduct[i + 1]) for i in range(rows - 1)
+    ]
+    below = [None] + [active[i] * faces[i - 1] for i in range(1, rows)]
+    above = [active[i] * faces[i] for i in range(rows - 1)] + [None]
+    scales, products, inverses = [], [], []
     for i in range(rows):
-        if i > 0:
-            gain = active[i] * face * inverses[-1]
-            gains.append(gain)
-            excess = 1.0 + gain * excess
-        if i < rows - 1:
-            face = (2.0 * implicit_ratio) * conduct[i] * conduct[i + 1] / (conduct[i] + conduct[i + 1])
-            upper = active[i] * face
-            inverse = 1.0 / (excess + upper)
-            backs.append(upper * inverse)
-        else:
-            inverse = 1.0 / excess
-            backs.append(None)
-        inverses.append(inverse)
+        diagonal = 1.0 + (above[i] if i == 0 else below[i] if i == rows - 1 else below[i] + above[i])
+        scales.append(1.0 / diagonal)
+    excess = scales[0]
+    products.append(jnp.ones_like(excess))
+    for i in range(1, rows):
+        excess = scales[i] * products[-1] + (scales[i] * below[i]) * excess
+        products.append(excess if i == rows - 1 else excess + (scales[i] * above[i]) * products[-1])
+    inverses = [scales[0]] + [scales[i] * products[i - 1] / products[i] for i in range(1, rows)]
+    gains = [None] + [below[i] * inverses[i - 1] for i in range(1, rows)]
+    backs = [above[i] * inverses[i] for i in range(rows - 1)] + [None]
     return gains, inverses, backs
 
 
@@ -107,8 +107,8 @@
     columns = hb.shape[1]
     tiles = columns // LANES
     field = tests * rows
-    copies[0].wait()
-    copies[1].wait()
+    for copy in copies:
+        copy.wait()
     conduct = jnp.exp(logk[...])
     active = (1 - mask[...]).astype(jnp.float32)
     for k in range(tiles):
@@ -132,8 +132,6 @@
     last_end = last[-1] + half / cond_rows[-1]
     across = first[-1]
 
-    copies[2].wait()
-    copies[3].wait()
     lane = lax.broadcasted_iota(jnp.int32, (rows, columns), 1)
     cond_north = pltpu.roll(conduct, columns - 1, 1)
     face = (2.0 * explicit_ratio) * conduct * cond_north / (conduct + cond_north)
@@ -149,24 +147,32 @@
             there = slice(k * field + rows * t, k * field + rows * (t + 1))
             right[there, :] = value[:, lanes]
             weighed[there, :] = seeded[:, lanes]
-    copies[4].wait()
-    copies[5].wait()
     row_start = lax.axis_index("gx") * rows
     column_start = lax.axis_index("gy") * columns
     row_lane = lax.broadcasted_iota(jnp.int32, (1, LANES), 1)
+    shift = total_columns.bit_length() - 1
+    places = []
     for t in range(tests):
-        well = wells[t]
-        well_row = well // total_columns - row_start
-        well_column = well % total_columns - column_start
+        if total_columns == 1 << shift:
+            well_row = lax.shift_right_logical(wells[t], shift)
+        else:
+            well_row = wells[t] // total_columns
+        well_column = wells[t] - well_row * total_columns - column_start
+        well_row = well_row - row_start
         inside = (well_row >= 0) & (well_row < rows) & (well_column >= 0) & (well_column < columns)
-
-        @pl.when(inside)
-        def _():
-            tile = well_column // LANES
-            act_row = act_c[pl.ds(tiles * well_row + tile, 1), :]
-            there = pl.ds(tile * field + rows * t + well_row, 1)
-            added = jnp.where(row_lane == well_column % LANES, act_row * rates[t], 0.0)
-            right[there, :] = right[there, :] + added
+        places.append((inside, well_row, well_column))
+
+    @pl.when(functools.reduce(jnp.logical_or, [inside for inside, _, _ in places]))
+    def _():
+        for t, (inside, well_row, well_column) in enumerate(places):
+
+            @pl.when(inside)
+            def _():
+                tile = well_column // LANES
+                act_row = act_c[pl.ds(tiles * well_row + tile, 1), :]
+                there = pl.ds(tile * field + rows * t + well_row, 1)
+                added = jnp.where(row_lane == well_column % LANES, act_row * rates[t], 0.0)
+                right[there, :] = right[there, :] + added
 
     for k in range(tiles):
         lanes = slice(k * LANES, (k + 1) * LANES)
@@ -198,18 +204,18 @@
     load = [None] + [last_value[i - 1] - first_value[i] for i in range(1, count)]
     middle = count // 2
     inverse = [None] * count
-    for i in range(1, middle):
-        if i > 1:
-            factor = across[i - 1] * inverse[i - 1]
-            diag[i] = diag[i] - factor * across[i - 1]
-            load[i] = load[i] + factor * load[i - 1]
-        inverse[i] = 1.0 / diag[i]
-    for i in range(count - 1, middle, -1):
-        if i < count - 1:
-            factor = across[i] * inverse[i + 1]
-            diag[i] = diag[i] - factor * across[i]
-            load[i] = load[i] + factor * load[i + 1]
-        inverse[i] = 1.0 / diag[i]
+    reciprocal = [None] + [1.0 / diag[i] for i in range(1, count)]
+    loss = [None] + [(across[i] * reciprocal[i]) * (across[i] * reciprocal[i + 1]) for i in range(1, count - 1)]
+    for order in (range(1, middle), range(count - 1, middle, -1)):
+        before = last = jnp.ones_like(diag[1])
+        previous = None
+        for i in order:
+            if previous is not None:
+                before, last = last, last - loss[min(i, previous)] * before
+            inverse[i] = reciprocal[i] if previous is None else reciprocal[i] * before / last
+            if previous is not None:
+                load[i] = load[i] + (across[min(i, previous)] * inverse[previous]) * load[previous]
+            previous = i
     below = across[middle - 1] * inverse[middle - 1]
     above = across[middle] * inverse[middle + 1]
     diag[middle] = diag[middle] - below * across[middle - 1] - above * across[middle]

time: 45.2 us -> 44.9 us (level)
  no operation moved by 1% of the time
where the time goes in v5:
time: 44.9 us; the launch traced here: 44.7 us
  starting transfers between devices  20.8 us (46%)
  blocking collectives  17.3 us (39%)
  Pallas kernels  5.08 us (11%)
  waiting for transfers between devices  0.77 us (2%)
  between operations  0.67 us (1%)
    all_to_all x1, blocking collectives, exchanged(): return lax.all_to_all(flat, 'gx', 0, 0).reshape(rows_of_all.shape)  17.3 us
    ppermute x1, starting transfers between devices, per_device(): lax.ppermute(to_left, 'gy', [(i + 1, i) for i in range(peers - 1)])  8.89 us
    all_to_all x1, starting transfers between devices, exchanged(): return lax.all_to_all(flat, 'gx', 0, 0).reshape(rows_of_all.shape)  7.93 us
    ppermute x1, starting transfers between devices, per_device(): lax.ppermute(to_right, 'gy', [(i, i + 1) for i in range(peers - 1)])  4.02 us
    pallas_call x1, Pallas kernels, per_device(): pl.pallas_call(functools.partial(local_kernel, rows, tests, columns * pee...  3.21 us
    pallas_call x1, Pallas kernels, per_device(): pl.pallas_call(functools.partial(final_kernel, rows, tests), in_specs=[VM...  1.59 us
  transfers between devices with their start and end apart: 3, of which 1 were waited for; matrix products, arithmetic and copies ran while one was open for 0% of the time, Pallas kernels for 0%

profile of v5, /device:TPU:7, one launch (start us, length us, event | category | flops | bytes accessed | tf_op | source)
XLA Modules:
  0.0 44.7 jit_solution(3142948137174397260)
XLA Ops:
  0.6 3.2 %local.1 = (f32[304,128]{1,0:T(8,128)}, f32[1024,128]{1,0:T(8,128)S(1)}, f32[1024,128]{1,0:T(8,128)S(1)}, f32[16,1024]{1,0:T(8,128)S(1)}, f32[16,1024]{1,0:T(8,1...) custom-call(s32[8]{0:T(128)} %wells_all.1, f32[8]{0:T(128)} %rates_all.1, ...), custom_call_target="tpu_custom_call" | custom-call | tf_op jit(solution)/shard_map/local/pallas_call | solution.py:402
  3.8 0.0 copy-start
  3.9 7.9 %all-to-all-start = ((f32[16,1,2432]{2,1,0:T(1,128)}), f32[16,1,2432]{2,1,0:T(1,128)S(1)}, u32[]{:S(2)}, u32[]{:S(2)}) async-start(f32[16,1,2432]{2,1,0:T(1,128)} %bitcast.2), calls=%async_computation | async-start | bytes 311296 | tf_op jit(solution)/shard_map/all_to_all | solution.py:399
  11.8 4.0 %collective-permute-start = (f32[16,128]{1,0:T(8,128)S(1)}, f32[16,128]{1,0:T(8,128)S(1)}, u32[]{:S(2)}, u32[]{:S(2)}) collective-permute-start(f32[16,128]{1,0:T(8,128)S(1)} %get-tuple-element.21), channel_id=1, source_target_pairs={{0,1},{1,2},{2,3},{3,4},{4,5},{5,6},{6,7},{7,8},{8,9},{9,10},{10,1... | collective-permute-start | bytes 24584 | tf_op jit(solution)/shard_map/ppermute | solution.py:419
  15.8 8.9 %collective-permute-start.1 = (f32[16,128]{1,0:T(8,128)S(1)}, f32[16,128]{1,0:T(8,128)S(1)}, u32[]{:S(2)}, u32[]{:S(2)}) collective-permute-start(f32[16,128]{1,0:T(8,128)S(1)} %get-tuple-element.22), channel_id=1, source_target_pairs={{1,0},{2,1},{3,2},{4,3},{5,4},{6,5},{7,6},{8,7},{9,8},{10,9},{11,1... | collective-permute-start | bytes 24584 | tf_op jit(solution)/shard_map/ppermute | solution.py:418
  24.7 0.0 collective-permute-done.from_left
  24.7 0.8 %collective-permute-done.1.from_right = f32[16,128]{1,0:T(8,128)S(1)} collective-permute-done((f32[16,128]{1,0:T(8,128)S(1)}, f32[16,128]{1,0:T(8,128)S(1)}, u32[]{:S(2)}, u32[]{:S(2)}) %collective-permute-start.1) | collective-permute-done | bytes 8224 | tf_op jit(solution)/shard_map/ppermute | solution.py:418
  25.5 0.0 all-to-all-done
  25.5 0.3 line.1
  25.8 0.0 copy-start.1
  25.8 17.3 %all_to_all.10 = f32[16,1,2304]{2,1,0:T(1,128)S(1)} all-to-all(f32[16,1,2304]{2,1,0:T(1,128)S(1)} %bitcast.11), channel_id=1, replica_groups=mesh['gx'=16,'gy'=32] {'gx'}, dimensions={0} | all-to-all | bytes 294912 | tf_op jit(solution)/shard_map/all_to_all | solution.py:399
  43.1 0.0 copy-done
  43.1 0.0 copy-done.1
  43.1 1.6 %final.1 = (f32[128,1024]{1,0:T(8,128)}, f32[16,1024]{1,0:T(8,128)}) custom-call(f32[128,1024]{1,0:T(8,128)S(1)} %bitcast.8, f32[16,1024]{1,0:T(8,128)S(1)} %copy-done.1, f32[1024,128]{1,0:T(8,128)S(1)} %get-tuple-element.16.heads_part, f32[1024,128]{1,0:T(8,128)S(1)} %get-tuple-element.17.adjoint_part, f32[16,1024]{1,0:T(8,128)S(1)} %get-tuple-element.18.first_in, ...), custom_call_target="tpu_custom_call" | custom-call | tf_op jit(solution)/shard_map/final/pallas_call | solution.py:429
Async XLA Ops:
  3.8 39.2 %copy-start = (f32[8,16,1024]{2,1,0:T(8,128)S(1)}, f32[8,16,1024]{2,1,0:T(8,128)}, u32[]{:S(2)}) copy-start(f32[8,16,1024]{2,1,0:T(8,128)} %param.6) | copy-start | bytes 1572868
  3.9 21.6 %all-to-all-start = ((f32[16,1,2432]{2,1,0:T(1,128)}), f32[16,1,2432]{2,1,0:T(1,128)S(1)}, u32[]{:S(2)}, u32[]{:S(2)}) async-start(f32[16,1,2432]{2,1,0:T(1,128)} %bitcast.2), calls=%async_computation | async-start | bytes 311296 | tf_op jit(solution)/shard_map/all_to_all | solution.py:399
  11.8 12.9 %collective-permute-start = (f32[16,128]{1,0:T(8,128)S(1)}, f32[16,128]{1,0:T(8,128)S(1)}, u32[]{:S(2)}, u32[]{:S(2)}) collective-permute-start(f32[16,128]{1,0:T(8,128)S(1)} %get-tuple-element.21), channel_id=1, source_target_pairs={{0,1},{1,2},{2,3},{3,4},{4,5},{5,6},{6,7},{7,8},{8,9},{9,10},{10,1... | collective-permute-start | bytes 24584 | tf_op jit(solution)/shard_map/ppermute | solution.py:419
  15.8 9.7 %collective-permute-start.1 = (f32[16,128]{1,0:T(8,128)S(1)}, f32[16,128]{1,0:T(8,128)S(1)}, u32[]{:S(2)}, u32[]{:S(2)}) collective-permute-start(f32[16,128]{1,0:T(8,128)S(1)} %get-tuple-element.22), channel_id=1, source_target_pairs={{1,0},{2,1},{3,2},{4,3},{5,4},{6,5},{7,6},{8,7},{9,8},{10,9},{11,1... | collective-permute-start | bytes 24584 | tf_op jit(solution)/shard_map/ppermute | solution.py:418
  25.8 17.3 %copy-start.1 = (f32[16,1024]{1,0:T(8,128)S(1)}, f32[16,1024]{1,0:T(8,128)}, u32[]{:S(2)}) copy-start(f32[16,1024]{1,0:T(8,128)} %logk.1) | copy-start | bytes 196612

commit v6 on v5

--- a/solution.py
+++ b/solution.py
@@ -258,26 +258,34 @@
     return ends
 
 
-def line_kernel(devices, rows, tests, got, from_left, from_right, own, reply, side_part, side_first, side_last):
-    out_rows, back_rows = 2 * tests + 3, 2 * tests + 2
-
-    def pick(low, high):
-        return [got[out_rows * d + low : out_rows * d + high, :] for d in range(devices)]
-
-    ends = [pick(2 * tests + r, 2 * tests + r + 1) for r in range(3)]
-    flux = chain(*ends, pick(0, tests), pick(tests, 2 * tests))
+def keep_kernel(given, out):
+    out[...] = given[...]
+
+
+def side_kernel(rows, tests, from_left, from_right, own, side_part, side_first, side_last, side_rows):
     side = side_lanes(rows, tests, from_left, from_right, own, side_part, side_first, side_last)
     width = 4 * tests
     lane = lax.broadcasted_iota(jnp.int32, (1, LANES), 1)
     joined = side[0]
     for r in range(1, 4):
         joined = jnp.where(lane >= width * r, pltpu.roll(side[r], width * r, 1), joined)
+    side_rows[0:1, :] = joined
+    side_rows[1:2, :] = side[4]
+
+
+def line_kernel(devices, tests, got, side_rows, reply):
+    out_rows, back_rows = 2 * tests + 3, 2 * tests + 2
+
+    def pick(low, high):
+        return [got[out_rows * d + low : out_rows * d + high, :] for d in range(devices)]
+
+    ends = [pick(2 * tests + r, 2 * tests + r + 1) for r in range(3)]
+    flux = chain(*ends, pick(0, tests), pick(tests, 2 * tests))
     for d in range(devices):
         start = back_rows * d
         reply[start : start + tests, :] = flux[d]
         reply[start + tests : start + 2 * tests, :] = flux[d + 1]
-        reply[start + 2 * tests : start + 2 * tests + 1, :] = joined
-        reply[start + 2 * tests + 1 : start + back_rows, :] = side[4]
+        reply[start + 2 * tests : start + back_rows, :] = side_rows[0:2, :]
 
 
 def final_kernel(
@@ -378,6 +386,8 @@
 
 
 VMEM = pl.BlockSpec(memory_space=pltpu.VMEM)
+SIDE_COST = 1000
+KEEP_COST = 7000000000
 PARAMS = pltpu.CompilerParams(vmem_limit_bytes=40 * 1024 * 1024)
 
 
@@ -417,14 +427,32 @@
     got = exchanged(message)
     from_right = lax.ppermute(to_left, "gy", [(i + 1, i) for i in range(peers - 1)])
     from_left = lax.ppermute(to_right, "gy", [(i, i + 1) for i in range(peers - 1)])
-    reply, side_part, side_first, side_last = pl.pallas_call(
-        functools.partial(line_kernel, devices, rows, tests),
-        in_specs=[VMEM] * 4,
+    from_left = pl.pallas_call(
+        keep_kernel,
+        in_specs=[VMEM],
+        out_specs=VMEM,
+        out_shape=side,
+        compiler_params=PARAMS,
+        cost_estimate=pl.CostEstimate(flops=KEEP_COST, bytes_accessed=0, transcendentals=0),
+        name="keep",
+    )(from_left)
+    side_part, side_first, side_last, side_rows = pl.pallas_call(
+        functools.partial(side_kernel, rows, tests),
+        in_specs=[VMEM] * 3,
         out_specs=[VMEM] * 4,
-        out_shape=[f32(devices * back_rows, LANES)] + [side] * 3,
+        out_shape=[side] * 3 + [f32(SUBLANES, LANES)],
+        compiler_params=PARAMS,
+        cost_estimate=pl.CostEstimate(flops=SIDE_COST, bytes_accessed=0, transcendentals=0),
+        name="sides",
+    )(from_left, from_right, own)
+    reply = pl.pallas_call(
+        functools.partial(line_kernel, devices, tests),
+        in_specs=[VMEM] * 2,
+        out_specs=VMEM,
+        out_shape=f32(devices * back_rows, LANES),
         compiler_params=PARAMS,
         name="line",
-    )(got, from_left, from_right, own)
+    )(got, side_rows)
     answer = exchanged(reply)
     heads, sensitivity = pl.pallas_call(
         functools.partial(final_kernel, rows, tests),

time: 44.9 us -> 44.9 us (level)
  transfers between devices with their start and end apart: 3 -> 3, of which waited for: 1 -> 1; matrix products, arithmetic and copies ran while one was open for 0% -> 0% of each run, Pallas kernels for 0% -> 1%
where the time goes in v6:
time: 44.9 us; the launch traced here: 44.6 us
  starting transfers between devices  20.7 us (46%)
  blocking collectives  17.3 us (39%)
  Pallas kernels  5.15 us (11%)
  waiting for transfers between devices  0.74 us (2%)
  between operations  0.69 us (2%)
    all_to_all x1, blocking collectives, exchanged(): return lax.all_to_all(flat, 'gx', 0, 0).reshape(rows_of_all.shape)  17.3 us
    ppermute x1, starting transfers between devices, per_device(): lax.ppermute(to_left, 'gy', [(i + 1, i) for i in range(peers - 1)])  8.59 us
    all_to_all x1, starting transfers between devices, exchanged(): return lax.all_to_all(flat, 'gx', 0, 0).reshape(rows_of_all.shape)  8.08 us
    ppermute x1, starting transfers between devices, per_device(): lax.ppermute(to_right, 'gy', [(i, i + 1) for i in range(peers - 1)])  4 us
    pallas_call x1, Pallas kernels, per_device(): pl.pallas_call(functools.partial(local_kernel, rows, tests, columns * pee...  3.21 us
    pallas_call x1, Pallas kernels, per_device(): pl.pallas_call(functools.partial(final_kernel, rows, tests), in_specs=[VM...  1.6 us
  transfers between devices with their start and end apart: 3, of which 1 were waited for; matrix products, arithmetic and copies ran while one was open for 0% of the time, Pallas kernels for 1%

profile of v6, /device:TPU:7, one launch (start us, length us, event | category | flops | bytes accessed | tf_op | source)
XLA Modules:
  0.0 44.6 jit_solution(15585956816101845372)
XLA Ops:
  0.6 3.2 %local.1 = (f32[304,128]{1,0:T(8,128)}, f32[1024,128]{1,0:T(8,128)S(1)}, f32[1024,128]{1,0:T(8,128)S(1)}, f32[16,1024]{1,0:T(8,128)S(1)}, f32[16,1024]{1,0:T(8,1...) custom-call(s32[8]{0:T(128)} %wells_all.1, f32[8]{0:T(128)} %rates_all.1, ...), custom_call_target="tpu_custom_call" | custom-call | tf_op jit(solution)/shard_map/local/pallas_call | solution.py:412
  3.8 4.0 %collective-permute-start = (f32[16,128]{1,0:T(8,128)S(1)}, f32[16,128]{1,0:T(8,128)S(1)}, u32[]{:S(2)}, u32[]{:S(2)}) collective-permute-start(f32[16,128]{1,0:T(8,128)S(1)} %get-tuple-element.21), channel_id=1, source_target_pairs={{0,1},{1,2},{2,3},{3,4},{4,5},{5,6},{6,7},{7,8},{8,9},{9,10},{10,1... | collective-permute-start | bytes 24584 | tf_op jit(solution)/shard_map/ppermute | solution.py:429
  7.9 8.1 %all-to-all-start = ((f32[16,1,2432]{2,1,0:T(1,128)}), f32[16,1,2432]{2,1,0:T(1,128)S(1)}, u32[]{:S(2)}, u32[]{:S(2)}) async-start(f32[16,1,2432]{2,1,0:T(1,128)} %bitcast.2), calls=%async_computation | async-start | bytes 311296 | tf_op jit(solution)/shard_map/all_to_all | solution.py:409
  15.9 8.6 %collective-permute-start.1 = (f32[16,128]{1,0:T(8,128)S(1)}, f32[16,128]{1,0:T(8,128)S(1)}, u32[]{:S(2)}, u32[]{:S(2)}) collective-permute-start(f32[16,128]{1,0:T(8,128)S(1)} %get-tuple-element.22), channel_id=1, source_target_pairs={{1,0},{2,1},{3,2},{4,3},{5,4},{6,5},{7,6},{8,7},{9,8},{10,9},{11,1... | collective-permute-start | bytes 24584 | tf_op jit(solution)/shard_map/ppermute | solution.py:428
  24.5 0.0 collective-permute-done.given
  24.6 0.0 copy-start
  24.6 0.7 %collective-permute-done.1.from_right = f32[16,128]{1,0:T(8,128)S(1)} collective-permute-done((f32[16,128]{1,0:T(8,128)S(1)}, f32[16,128]{1,0:T(8,128)S(1)}, u32[]{:S(2)}, u32[]{:S(2)}) %collective-permute-start.1) | collective-permute-done | bytes 8224 | tf_op jit(solution)/shard_map/ppermute | solution.py:428
  25.3 0.3 sides.1
  25.6 0.0 all-to-all-done
  25.6 0.1 line.1
  25.7 0.0 copy-start.1
  25.7 17.3 %all_to_all.10 = f32[16,1,2304]{2,1,0:T(1,128)S(1)} all-to-all(f32[16,1,2304]{2,1,0:T(1,128)S(1)} %bitcast.10), channel_id=1, replica_groups=mesh['gx'=16,'gy'=32] {'gx'}, dimensions={0} | all-to-all | bytes 294912 | tf_op jit(solution)/shard_map/all_to_all | solution.py:409
  43.0 0.0 copy-done
  43.0 0.0 copy-done.1
  43.0 1.6 %final.1 = (f32[128,1024]{1,0:T(8,128)}, f32[16,1024]{1,0:T(8,128)}) custom-call(f32[128,1024]{1,0:T(8,128)S(1)} %bitcast.8, f32[16,1024]{1,0:T(8,128)S(1)} %copy-done.1, f32[1024,128]{1,0:T(8,128)S(1)} %get-tuple-element.16.heads_part, f32[1024,128]{1,0:T(8,128)S(1)} %get-tuple-element.17.adjoint_part, f32[16,1024]{1,0:T(8,128)S(1)} %get-tuple-element.18.first_in, ...), custom_call_target="tpu_custom_call" | custom-call | tf_op jit(solution)/shard_map/final/pallas_call | solution.py:457
  (1 shorter events, 0.0 us)
Async XLA Ops:
  3.8 20.7 %collective-permute-start = (f32[16,128]{1,0:T(8,128)S(1)}, f32[16,128]{1,0:T(8,128)S(1)}, u32[]{:S(2)}, u32[]{:S(2)}) collective-permute-start(f32[16,128]{1,0:T(8,128)S(1)} %get-tuple-element.21), channel_id=1, source_target_pairs={{0,1},{1,2},{2,3},{3,4},{4,5},{5,6},{6,7},{7,8},{8,9},{9,10},{10,1... | collective-permute-start | bytes 24584 | tf_op jit(solution)/shard_map/ppermute | solution.py:429
  7.9 17.7 %all-to-all-start = ((f32[16,1,2432]{2,1,0:T(1,128)}), f32[16,1,2432]{2,1,0:T(1,128)S(1)}, u32[]{:S(2)}, u32[]{:S(2)}) async-start(f32[16,1,2432]{2,1,0:T(1,128)} %bitcast.2), calls=%async_computation | async-start | bytes 311296 | tf_op jit(solution)/shard_map/all_to_all | solution.py:409
  15.9 9.4 %collective-permute-start.1 = (f32[16,128]{1,0:T(8,128)S(1)}, f32[16,128]{1,0:T(8,128)S(1)}, u32[]{:S(2)}, u32[]{:S(2)}) collective-permute-start(f32[16,128]{1,0:T(8,128)S(1)} %get-tuple-element.22), channel_id=1, source_target_pairs={{1,0},{2,1},{3,2},{4,3},{5,4},{6,5},{7,6},{8,7},{9,8},{10,9},{11,1... | collective-permute-start | bytes 24584 | tf_op jit(solution)/shard_map/ppermute | solution.py:428
  24.6 18.4 %copy-start = (f32[8,16,1024]{2,1,0:T(8,128)S(1)}, f32[8,16,1024]{2,1,0:T(8,128)}, u32[]{:S(2)}) copy-start(f32[8,16,1024]{2,1,0:T(8,128)} %param.6) | copy-start | bytes 1572868
  25.7 17.3 %copy-start.1 = (f32[16,1024]{1,0:T(8,128)S(1)}, f32[16,1024]{1,0:T(8,128)}, u32[]{:S(2)}) copy-start(f32[16,1024]{1,0:T(8,128)} %logk.1) | copy-start | bytes 196612
